TPU v7x, 128 devices: a whole 4x4x4 slice. The times are simulated.
128 devices in a mesh: gx: 2 (over core), gy: 8 (over y_lo, x), gz: 8 (over y_hi, z).
Axes of the slice: x: 4, y: 4 (y_hi: 2, y_lo: 2; y = y_hi * 2 + y_lo), z: 4, core: 2. Of those that a mesh axis runs over, the one named last changes fastest.
Arguments:
- inputs: bfloat16 [1280, 6144], P('gx', ('gy', 'gz')), may hold values from -6 to 6
- out_grad: bfloat16 [1280, 6144], P('gx', ('gy', 'gz')), may hold values from -6 to 6
- up_weight: bfloat16 [6144, 24576], P('gy', ('gx', 'gz')), may hold values from -0.078125 to 0.078125
- down_weight: bfloat16 [24576, 6144], P(('gx', 'gz'), 'gy'), may hold values from -0.0390625 to 0.0390625
Outputs:
- in_grad: bfloat16 [1280, 6144], P('gx', ('gy', 'gz'))
- up_weight_grad: bfloat16 [6144, 24576], P('gy', ('gx', 'gz'))
- down_weight_grad: bfloat16 [24576, 6144], P(('gx', 'gz'), 'gy')
All inputs are finite; a program needn't handle non-finite values.
Results may differ from a plain program's by a relative error of at most 0.005.
Values may be sent and summed in bfloat16 or wider, within the bound.
A program may use at most 128 MiB of HBM per device.

v0:
```python
import jax
import jax.numpy as jnp
from jax import lax
from jax.sharding import PartitionSpec as P

gelu_scale = 0.7978845608028654
cubic_term = 0.044715


def activate(hidden_pre, act_grad):
    inner = gelu_scale * (hidden_pre + cubic_term * hidden_pre * hidden_pre * hidden_pre)
    tanh_val = jnp.tanh(inner)
    activation = 0.5 * hidden_pre * (1.0 + tanh_val)
    deriv = 0.5 * (1.0 + tanh_val) + 0.5 * hidden_pre * (1.0 - tanh_val * tanh_val) * gelu_scale * (
        1.0 + 3.0 * cubic_term * hidden_pre * hidden_pre
    )
    return (activation.astype(jnp.bfloat16), (act_grad * deriv).astype(jnp.bfloat16))


def contract_dims(left, right, left_dim, right_dim):
    return lax.dot_general(
        left, right, (((left_dim,), (right_dim,)), ((), ())), preferred_element_type=jnp.float32
    )


def width_shares(partial_grad):
    return lax.psum_scatter(partial_grad, "gz", scatter_dimension=1, tiled=True)


def body(inputs, out_grad, up_weight, down_weight):
    input_cols, grad_cols = (
        lax.all_gather(inputs, "gz", axis=1, tiled=True),
        lax.all_gather(out_grad, "gz", axis=1, tiled=True),
    )
    up_all, down_all = (
        lax.all_gather(up_weight, "gx", axis=1, tiled=True),
        lax.all_gather(down_weight, "gx", axis=0, tiled=True),
    )
    input_rows, grad_rows = (input_cols, grad_cols)
    pre_part = jnp.dot(input_rows, up_all, preferred_element_type=jnp.float32)
    back_part = contract_dims(grad_rows, down_all, 1, 1)
    hidden_pre, act_grad = lax.psum((pre_part, back_part), "gy")
    activation, pre_grad = activate(hidden_pre, act_grad)
    input_part = contract_dims(pre_grad, up_all, 1, 1)
    up_part = contract_dims(input_rows, pre_grad, 0, 0)
    in_grad = width_shares(input_part)
    up_weight_grad = lax.psum_scatter(up_part, "gx", scatter_dimension=1, tiled=True)
    down_weight_grad = lax.psum_scatter(
        contract_dims(activation, grad_rows, 0, 0), "gx", scatter_dimension=0, tiled=True
    )
    return (
        in_grad.astype(jnp.bfloat16),
        up_weight_grad.astype(jnp.bfloat16),
        down_weight_grad.astype(jnp.bfloat16),
    )


def solution(mesh):
    return jax.shard_map(
        body,
        mesh=mesh,
        in_specs=(
            P("gx", ("gy", "gz")),
            P("gx", ("gy", "gz")),
            P("gy", ("gx", "gz")),
            P(("gx", "gz"), "gy"),
        ),
        out_specs=(P("gx", ("gy", "gz")), P("gy", ("gx", "gz")), P(("gx", "gz"), "gy")),
        check_vma=False,
    )
```

profile of v0, /device:TPU:0, one launch (start us, length us, event | category | flops | bytes accessed | tf_op | source)
XLA Modules:
  0.0 570.7 jit_solution(17619005750293956113)
XLA Ops:
  7.2 0.0 all-gather.3.cloned.1.call-start
  7.2 0.7 all-gather.3.cloned.1.call-update
  7.9 0.0 all-gather.5.cloned.1.call-start
  7.9 0.7 all-gather.5.cloned.1.call-update
  8.6 0.0 all-reduce.3.cloned.1.call-start
  8.7 37.4 %all_gather.14 = bf16[640,768]{0,1:T(8,128)(2,1)S(1)} all-gather(bf16[640,96]{0,1:T(8,128)(2,1)} %param.4), channel_id=1, replica_groups=mesh['gx'=2,'gy'=8,'gz'=8] {'gz'}, dimensions={1}, use_global_device_ids=true | all-gather | bytes 1105920 | tf_op jit(solution)/shard_map/all_gather | solution.py:32
  46.1 36.6 %all_gather.12 = bf16[640,768]{0,1:T(8,128)(2,1)S(1)} all-gather(bf16[640,96]{0,1:T(8,128)(2,1)} %param.5), channel_id=1, replica_groups=mesh['gx'=2,'gy'=8,'gz'=8] {'gz'}, dimensions={1}, use_global_device_ids=true | all-gather | bytes 1105920 | tf_op jit(solution)/shard_map/all_gather | solution.py:33
  82.7 8.7 %fusion.16 = f32[640,3072]{1,0:T(8,128)} fusion(bf16[640,768]{0,1:T(8,128)(2,1)S(1)} %all_gather.12, bf16[3072,768]{1,0:T(8,128)(2,1)} %all-gather.3.cloned.1.call-done), kind=kOutput, calls=%fused_computation.20 | convolution fusion | flops 3019898880 | bytes 13565952 | tf_op jit(solution)/shard_map/dot_general | solution.py:21
  91.4 8.7 %fusion.17 = f32[640,3072]{1,0:T(8,128)} fusion(bf16[640,768]{0,1:T(8,128)(2,1)S(1)} %all_gather.14, bf16[768,3072]{1,0:T(8,128)(2,1)} %all-gather.5.cloned.1.call-done), kind=kOutput, calls=%fused_computation.21 | convolution fusion | flops 3019898880 | bytes 13565952 | tf_op jit(solution)/shard_map/dot_general | solution.py:40
  100.1 0.0 all-reduce.3.cloned.1.call-update
  100.1 0.0 reduce-scatter.4.cloned.1.call-start
  100.2 323.9 %all-reduce.3.cloned.1.call-done = (f32[640,3072]{1,0:T(8,128)}, f32[640,3072]{1,0:T(8,128)}) async-done(((f32[640,3072]{1,0:T(8,128)}, f32[640,3072]{1,0:T(8,128)}), (f32[640,3072]{1,0:T(8,128)}, f32[640,3072]{1,0:T(8,128)})) %all-reduce.3.cloned.1.call-update) | async-done | bytes 15728656 | tf_op jit(solution)/shard_map/psum | solution.py:42
  424.1 8.5 %fusion.6 = bf16[640,3072]{1,0:T(8,128)(2,1)S(1)} fusion(f32[640,3072]{1,0:T(8,128)} %get-tuple-element.6, f32[640,3072]{1,0:T(8,128)} %get-tuple-element.7), kind=kLoop, calls=%fused_computation.8 | loop fusion | flops 37355520 | bytes 19660800 | tf_op jit(solution)/shard_map/convert_element_type | solution.py:17
  432.7 0.0 copy-start
  432.7 1.9 copy-done
  434.6 0.0 slice-done
  434.6 0.0 slice-done.1
  434.6 5.1 fusion.18
  439.7 0.0 reduce-scatter.4.cloned.1.call-update
  439.7 0.2 reduce-scatter.6.cloned.1.call-start
  440.0 8.4 %convolution_bitcast_fusion = f32[768,3072]{0,1:T(8,128)} fusion(bf16[640,3072]{1,0:T(8,128)(2,1)} %copy-done, bf16[640,768]{0,1:T(8,128)(2,1)S(1)} %all_gather.14), kind=kOutput, calls=%fused_computation.10 | convolution fusion | flops 3019898880 | bytes 14352384 | tf_op jit(solution)/shard_map/dot_general | solution.py:21
  448.4 0.0 reduce-scatter.6.cloned.1.call-update
  448.4 0.0 reduce-scatter.8.cloned.1.call-start
  448.4 12.8 %fusion.7 = f32[3072,768]{1,0:T(8,128)} fusion(bf16[640,768]{0,1:T(8,128)(2,1)S(1)} %all_gather.12, f32[640,3072]{1,0:T(8,128)} %get-tuple-element.7), kind=kOutput, calls=%fused_computation.11 | convolution fusion | flops 3037593600 | bytes 18284544 | tf_op jit(solution)/shard_map/dot_general | solution.py:21
  461.2 0.0 reduce-scatter.8.cloned.1.call-update
  461.3 52.7 %reduce-scatter.4.cloned.1.call-done = f32[640,96]{0,1:T(8,128)} async-done(((f32[640,768]{0,1:T(8,128)}), f32[640,96]{0,1:T(8,128)}) %reduce-scatter.4.cloned.1.call-update) | async-done | bytes 245776 | tf_op jit(solution)/shard_map/reduce_scatter | solution.py:27
  513.9 1.6 convert_element_type.16
  515.5 20.0 %reduce-scatter.6.cloned.1.call-done = f32[768,1536]{0,1:T(8,128)} async-done(((f32[768,3072]{0,1:T(8,128)}), f32[768,1536]{0,1:T(8,128)}) %reduce-scatter.6.cloned.1.call-update) | async-done | bytes 4718608 | tf_op jit(solution)/shard_map/reduce_scatter | solution.py:47
  535.5 2.6 convert_element_type.17
  538.1 2.4 copy.7
  540.5 19.4 %reduce-scatter.8.cloned.1.call-done = f32[1536,768]{1,0:T(8,128)} async-done(((f32[3072,768]{1,0:T(8,128)}), f32[1536,768]{1,0:T(8,128)}) %reduce-scatter.8.cloned.1.call-update) | async-done | bytes 4718608 | tf_op jit(solution)/shard_map/reduce_scatter | solution.py:48
  559.9 4.0 convert_element_type.19
  (5 shorter events, 0.0 us)
Async XLA Ops:
  7.2 75.5 %all-gather.3.cloned.1.call-start = ((), (), s32[]{:S(2)}) async-start(), calls=%async_computation.3 | async-start | bytes 7077888 | tf_op jit(solution)/shard_map/all_gather | solution.py:37
  7.9 83.5 %all-gather.5.cloned.1.call-start = ((), (), s32[]{:S(2)}) async-start(), calls=%async_computation.4 | async-start | bytes 7077888 | tf_op jit(solution)/shard_map/all_gather | solution.py:36
  8.6 415.5 %all-reduce.3.cloned.1.call-start = ((), (), s32[]{:S(2)}) async-start(), calls=%async_computation.8 | async-start | bytes 31457280 | tf_op jit(solution)/shard_map/psum | solution.py:42
  100.1 334.5 %slice-start = ((s8[4718592]{0:T(1024)(128)(4,1)}), s8[524288]{0:T(1024)(128)(4,1)S(1)}, s32[]{:S(2)}) async-start(s8[4718592]{0:T(1024)(128)(4,1)} %bitcast.11), calls=%async_computation.9 | async-start | bytes 1048576
  100.1 413.8 %reduce-scatter.4.cloned.1.call-start = ((), (), s32[]{:S(2)}) async-start(), calls=%async_computation.5 | async-start | bytes 2211840 | tf_op jit(solution)/shard_map/reduce_scatter | solution.py:27
  424.1 10.4 %slice-start.1 = ((s8[4718592]{0:T(1024)(128)(4,1)}), s8[4194304]{0:T(1024)(128)(4,1)S(1)}, s32[]{:S(2)}) async-start(s8[4718592]{0:T(1024)(128)(4,1)} %bitcast.11), calls=%async_computation.10 | async-start | bytes 8388608
  432.7 1.9 copy-start
  439.7 95.8 %reduce-scatter.6.cloned.1.call-start = ((), (), s32[]{:S(2)}) async-start(), calls=%async_computation.6 | async-start | bytes 14155776 | tf_op jit(solution)/shard_map/reduce_scatter | solution.py:47
  448.4 111.5 %reduce-scatter.8.cloned.1.call-start = ((), (), s32[]{:S(2)}) async-start(), calls=%async_computation.7 | async-start | bytes 14155776 | tf_op jit(solution)/shard_map/reduce_scatter | solution.py:48
Sparse Core Ops, SparseCore 0:
  9.6 19.5 all-gather.2
  30.9 18.4 all-gather.4
  100.3 323.8 all-reduce.2
  439.9 74.0 reduce-scatter.3
  516.3 19.1 reduce-scatter.5
  537.9 21.9 reduce-scatter.7
where the time goes:
time: 572 us; the launch traced here: 571 us
  waiting for transfers between devices  417 us (73%)
  blocking collectives  74 us (13%)
  matrix products  43.7 us (8%)
  other arithmetic  16.7 us (3%)
  between operations  14.1 us (2%)
    psum x1, waiting for transfers between devices, body(): hidden_pre, act_grad = lax.psum((pre_part, back_part), 'gy')  324 us
    reduce_scatter x1, waiting for transfers between devices, width_shares(): return lax.psum_scatter(partial_grad, 'gz', scatter_dimension=1, tiled=True)  52.7 us
    all_gather x1, blocking collectives, body(): lax.all_gather(inputs, 'gz', axis=1, tiled=True)  37.4 us
    all_gather x1, blocking collectives, body(): lax.all_gather(out_grad, 'gz', axis=1, tiled=True)  36.6 us
    dot_general x4, matrix products, contract_dims(): lax.dot_general(left, right, (((left_dim,), (right_dim,)), ((), ())), pre...  35 us
    reduce_scatter x1, waiting for transfers between devices, body(): lax.psum_scatter(up_part, 'gx', scatter_dimension=1, tiled=True)  20 us
    reduce_scatter x1, waiting for transfers between devices, body(): lax.psum_scatter(contract_dims(activation, grad_rows, 0, 0), 'gx', scatte...  19.4 us
  transfers between devices with their start and end apart: 6, of which 4 were waited for; matrix products, arithmetic and copies ran while one was open for 6% of the time, Pallas kernels for 0%

commit v1 on v0

v1 whole, which is shorter than its diff:
```python
import functools

import jax
import jax.numpy as jnp
from jax import lax
from jax.experimental import pallas as pl
from jax.experimental.pallas import tpu as pltpu
from jax.sharding import PartitionSpec as P

gelu_scale = 0.7978845608028654
cubic_term = 0.044715

MESH = pl.DeviceIdType.MESH
BF16, F32 = jnp.bfloat16, jnp.float32

CHUNKS = ((0, 256), (256, 384))
SEMS = 90 * len(CHUNKS)


def nn(left, right):
    return jnp.dot(left, right, preferred_element_type=F32)


def nt(left, right):
    return lax.dot_general(left, right, (((1,), (1,)), ((), ())), preferred_element_type=F32)


def aligned(index, step):
    return pl.multiple_of(index * step, step)


class Place:
    def __init__(self):
        self.c = lax.axis_index("gx")
        self.gy = lax.axis_index("gy")
        self.gz = lax.axis_index("gz")
        self.yl, self.x = self.gy // 4, self.gy % 4
        self.yh, self.z = self.gz // 4, self.gz % 4

    def dev(self, dc=0, dyl=0, dx=0, dyh=0, dz=0):
        return (
            (self.c + dc) % 2,
            self.owner((self.yl + dyl) % 2, dx),
            self.zblock(dyh, dz),
        )

    def owner(self, row, dx):
        return row * 4 + (self.x + dx) % 4

    def zblock(self, dyh, dz):
        return ((self.yh + dyh) % 2) * 4 + (self.z + dz) % 4


class Net:
    def __init__(self, send_sems, recv_sems):
        self.send_sems, self.recv_sems = send_sems, recv_sems
        self.copies = []

    def send(self, src, dst, device):
        i = len(self.copies)
        assert i < SEMS
        copy = pltpu.make_async_remote_copy(
            src_ref=src,
            dst_ref=dst,
            send_sem=self.send_sems.at[i],
            recv_sem=self.recv_sems.at[i],
            device_id=device,
            device_id_type=MESH,
        )
        copy.start()
        self.copies.append(copy)
        return copy

    def drain(self):
        for copy in self.copies:
            copy.wait_send()


class Ring:
    def __init__(self, net, here, out, far, near, partial):
        self.net, self.out, self.far, self.near, self.partial = net, out, far, near, partial
        self.right, self.left = here.dev(dx=1), here.dev(dx=3)
        self.h = out.shape[1] // 2

    def half(self, i):
        return pl.ds(i * self.h, self.h)

    def push(self, slot, half, value, dst, device):
        src = self.out.at[slot, self.half(half)]
        src[...] = value.astype(BF16)
        return self.net.send(src, dst, device)

    def opposite(self):
        self.far_copies = [
            self.push(0, 0, self.partial(2, 0), self.far.at[0], self.right),
            self.push(0, 1, self.partial(2, 1), self.far.at[1], self.left),
        ]

    def beside(self):
        self.near_copies = [
            self.push(1, 1, self.partial(1, 1), self.near.at[0, self.half(1)], self.right),
            self.push(2, 0, self.partial(3, 0), self.near.at[1, self.half(0)], self.left),
        ]

    def relay(self):
        for i, (slot, dx, device) in enumerate(((1, 1, self.right), (2, 3, self.left))):
            part = self.partial(dx, i)
            self.far_copies[i].wait_recv()
            value = part + self.far[i].astype(F32)
            self.near_copies.append(
                self.push(slot, i, value, self.near.at[i, self.half(i)], device)
            )

    def arrive(self):
        for copy in self.near_copies:
            copy.wait_recv()

    def total(self, half):
        rows = self.half(half)
        return (
            self.partial(0, half)
            + self.near[0, rows].astype(F32)
            + self.near[1, rows].astype(F32)
        )


class YFirst:
    def __init__(self, net, here, bufs, weight, acts, block):
        self.net, self.here, self.bufs, self.block = net, here, bufs, block
        self.weight, self.acts = weight, acts
        self.waited = set()
        self.ring = Ring(net, here, bufs["out"].at[0], bufs["far"].at[0], bufs["near"].at[0], self.partial)

    def product(self, row, dx, half):
        h = self.block // 2
        first = aligned(self.here.owner(row, dx) * 2 + half, h)
        return nn(self.weight[pl.ds(first, h), :], self.acts[...])

    def partial(self, dx, half):
        if dx not in self.waited:
            self.y_copies[dx].wait_recv()
            self.waited.add(dx)
        h = self.block // 2
        return self.product(self.here.yl, dx, half) + self.bufs["y_in"][dx, pl.ds(half * h, h)].astype(F32)

    def start(self):
        self.y_copies = {}
        h = self.block // 2
        for dx in (2, 1, 3, 0):
            for half in range(2):
                self.bufs["y_out"][dx, pl.ds(half * h, h)] = self.product(1 - self.here.yl, dx, half).astype(BF16)
            self.y_copies[dx] = self.net.send(
                self.bufs["y_out"].at[dx], self.bufs["y_in"].at[dx], self.here.dev(dyl=1)
            )

    def second(self):
        self.ring.opposite()
        self.ring.beside()

    def third(self):
        self.ring.relay()

    def last(self):
        self.ring.arrive()

    def total(self, half):
        return self.ring.total(half)


class XFirst:
    def __init__(self, net, here, bufs, weight, acts, block):
        self.net, self.here, self.bufs, self.block = net, here, bufs, block
        self.weight, self.acts = weight, acts
        self.rings = [
            Ring(
                net, here, bufs["out"].at[i], bufs["far"].at[i], bufs["near"].at[i],
                functools.partial(self.product, row),
            )
            for i, row in enumerate((1 - here.yl, here.yl))
        ]

    product = YFirst.product

    def start(self):
        for ring in self.rings:
            ring.opposite()
        for ring in self.rings:
            ring.beside()

    def second(self):
        for ring in self.rings:
            ring.relay()

    def third(self):
        self.rings[0].arrive()
        h = self.block // 2
        for half in range(2):
            self.bufs["y_out"][0, pl.ds(half * h, h)] = self.rings[0].total(half).astype(BF16)
        self.y_copy = self.net.send(
            self.bufs["y_out"].at[0], self.bufs["y_in"].at[0], self.here.dev(dyl=1)
        )

    def last(self):
        self.rings[1].arrive()
        self.y_copy.wait_recv()

    def total(self, half):
        h = self.block // 2
        return self.rings[1].total(half) + self.bufs["y_in"][0, pl.ds(half * h, h)].astype(F32)


class Share:
    def __init__(self, net, here, buf, row, block):
        self.net, self.here, self.buf, self.row, self.block = net, here, buf, row, block
        self.h = block // 2
        self.right, self.left = here.dev(dx=1), here.dev(dx=3)

    def ref(self, dx, half=None):
        owner = self.here.owner(self.row, dx)
        if half is None:
            return self.buf.at[pl.ds(aligned(owner, self.block), self.block)]
        return self.buf.at[pl.ds(aligned(owner * 2 + half, self.h), self.h)]

    def push(self, ref, device):
        return self.net.send(ref, ref, device)

    def start(self):
        first = [self.push(self.ref(0, 0), self.right), self.push(self.ref(0, 1), self.left)]
        second = [self.push(self.ref(0, 1), self.right), self.push(self.ref(0, 0), self.left)]
        self.first, self.second = first, second

    def relay(self):
        self.first[0].wait_recv()
        self.far = [self.push(self.ref(3, 0), self.right)]
        self.first[1].wait_recv()
        self.far.append(self.push(self.ref(1, 1), self.left))

    def arrive_near(self):
        for copy in self.second:
            copy.wait_recv()

    def arrive_far(self):
        for copy in self.far:
            copy.wait_recv()


class ShareXFirst:
    def __init__(self, net, here, buf, block):
        self.net, self.here = net, here
        self.ring = Share(net, here, buf, here.yl, block)

    def over(self, dx):
        ref = self.ring.ref(dx)
        self.y_copies.append(self.net.send(ref, ref, self.here.dev(dyl=1)))

    def start(self):
        self.y_copies = []
        self.ring.start()
        self.over(0)

    def second(self):
        self.ring.relay()
        self.ring.arrive_near()
        self.over(1)
        self.over(3)

    def third(self):
        self.ring.arrive_far()
        self.over(2)

    def own_row(self):
        pass

    def other_row(self):
        for copy in self.y_copies:
            copy.wait_recv()


class ShareYFirst:
    def __init__(self, net, here, buf, block):
        self.net, self.here = net, here
        self.rings = [Share(net, here, buf, row, block) for row in (here.yl, 1 - here.yl)]

    def start(self):
        ref = self.rings[0].ref(0)
        self.y_copy = self.net.send(ref, ref, self.here.dev(dyl=1))
        self.rings[0].start()

    def second(self):
        self.y_copy.wait_recv()
        self.rings[1].start()
        self.rings[0].relay()

    def third(self):
        self.rings[1].relay()

    def own_row(self):
        self.rings[0].arrive_near()
        self.rings[0].arrive_far()

    def other_row(self):
        self.rings[1].arrive_near()
        self.rings[1].arrive_far()


class Chunk:
    def __init__(self, index, net, here, bufs, shared):
        self.first, self.size = CHUNKS[index]
        self.is_first, self.is_last = index == 0, index == len(CHUNKS) - 1
        self.net, self.here, self.bufs, self.shared = net, here, bufs, shared

    def feature_ref(self, zblock, core):
        return self.bufs["acts"].at[
            :, pl.ds(aligned(zblock, 96), 96), pl.ds(aligned(core, self.size), self.size)
        ]

    def pass_on(self, zblock, device):
        ref = self.feature_ref(zblock, self.here.c)
        return self.net.send(ref, ref, device)

    def load(self):
        here = self.here
        for i, name in enumerate(("inputs", "out_grad")):
            block = self.shared[name][pl.ds(self.first, self.size), :]
            self.bufs["acts"][
                i, pl.ds(aligned(here.gz, 96), 96), pl.ds(aligned(here.c, self.size), self.size)
            ] = block.T

    def gather_start(self):
        here = self.here
        self.y_copy = self.pass_on(here.gz, here.dev(dyh=1))
        self.z_copies = [self.pass_on(here.gz, here.dev(dz=dz)) for dz in (1, 3, 2)]
        self.core_copies = [self.pass_on(here.gz, here.dev(dc=1))]

    def gather_second(self):
        here = self.here
        self.y_copy.wait_recv()
        block = here.zblock(1, 0)
        self.z_copies += [self.pass_on(block, here.dev(dz=dz)) for dz in (1, 3, 2)]
        self.core_copies.append(self.pass_on(block, here.dev(dc=1)))

    def gather_third(self):
        here = self.here
        for i, copy in enumerate(self.z_copies):
            copy.wait_recv()
            block = here.zblock(i // 3, (3, 1, 2)[i % 3])
            self.core_copies.append(self.pass_on(block, here.dev(dc=1)))

    def gather_last(self):
        for copy in self.core_copies:
            copy.wait_recv()

    def sum_start(self):
        block = self.shared["block"]
        args = (self.net, self.here)
        acts = self.bufs["acts"]
        self.pre = YFirst(*args, self.bufs["pre"], self.shared["up_t"], acts.at[0], block)
        self.back = XFirst(*args, self.bufs["back"], self.shared["down"], acts.at[1], block)
        self.back.start()
        self.pre.start()

    def sum_second(self):
        self.back.second()
        self.pre.second()

    def sum_third(self):
        self.back.third()
        self.pre.third()

    def activate(self):
        self.back.last()
        self.pre.last()
        hidden, back = self.bufs["hidden"], self.bufs["hidden_back"]
        block = self.shared["block"]
        h = block // 2
        for half in range(2):
            hidden[pl.ds(half * h, h), :] = self.pre.total(half)
            back[pl.ds(half * h, h), :] = self.back.total(half)
        base = self.here.gy * block

        @pl.loop(0, block // 16)
        def _(i):
            rows = pl.ds(pl.multiple_of(i * 16, 16), 16)
            to = pl.ds(pl.multiple_of(base + i * 16, 16), 16)
            x = hidden[rows, :]
            t = jnp.tanh(gelu_scale * (x + cubic_term * x * x * x))
            deriv = 0.5 * (1.0 + t) + 0.5 * x * (1.0 - t * t) * gelu_scale * (1.0 + 3.0 * cubic_term * x * x)
            self.bufs["activation"][to, :] = (0.5 * x * (1.0 + t)).astype(BF16)
            self.bufs["pre_grad"][to, :] = (back[rows, :] * deriv).astype(BF16)

    def share_start(self):
        block = self.shared["block"]
        self.act_share = ShareXFirst(self.net, self.here, self.bufs["activation"], block)
        self.grad_share = ShareYFirst(self.net, self.here, self.bufs["pre_grad"], block)
        self.grad_share.start()
        self.act_share.start()

    def share_second(self):
        self.grad_share.second()
        self.act_share.second()

    def share_third(self):
        self.grad_share.third()
        self.act_share.third()

    def in_grad_rows(self, row, add):
        up, pre_grad, total = self.shared["up"], self.bufs["pre_grad"], self.bufs["in_grad"]
        cols = pl.ds(aligned(row, 768), 768)

        @pl.loop(0, 3)
        def _(i):
            rows = pl.ds(pl.multiple_of(i * 256, 256), 256)
            value = nn(up[rows, cols], pre_grad[cols, :])
            total[rows, :] = total[rows, :] + value if add else value

    def weight_grads(self, row):
        acts, pre_grad, activation = self.bufs["acts"], self.bufs["pre_grad"], self.bufs["activation"]
        shared = self.shared
        cols = pl.ds(aligned(row, 768), 768)

        def put(total, stage, rows, cols, value):
            if not self.is_first:
                value = value + total[rows, cols]
            if self.is_last:
                stage[rows, cols] = value.astype(BF16)
            else:
                total[rows, cols] = value

        @pl.loop(0, 3)
        def _(i):
            rows = pl.ds(pl.multiple_of(i * 256, 256), 256)
            put(
                shared["up_total"], shared["up_stage"], rows, cols,
                nt(acts[0, rows, :], pre_grad[cols, :]),
            )

        if self.is_last:
            part = (slice(None), cols)
            self.flush(shared["up_stage"].at[part], shared["up_grad"].at[part])

        @pl.loop(0, 3)
        def _(i):
            rows = pl.ds(pl.multiple_of(row * 768 + i * 256, 256), 256)
            put(
                shared["down_total"], shared["down_stage"], rows, slice(None),
                nt(activation[rows, :], acts[1]),
            )

        if self.is_last:
            self.flush(shared["down_stage"].at[cols], shared["down_grad"].at[cols])

    def flush(self, src, dst):
        i = len(self.shared["flushes"])
        copy = pltpu.make_async_copy(src, dst, self.shared["local_sems"].at[i])
        copy.start()
        self.shared["flushes"].append(copy)

    def reduce_start(self):
        here = self.here
        theirs = pl.ds(aligned(1 - here.c, self.size), self.size)
        self.core_copy = self.net.send(
            self.bufs["in_grad"].at[:, theirs], self.bufs["in_grad_core"], here.dev(dc=1)
        )

    def core_sum(self, zblock):
        rows = pl.ds(aligned(zblock, 96), 96)
        mine = pl.ds(aligned(self.here.c, self.size), self.size)
        return self.bufs["in_grad"][rows, mine] + self.bufs["in_grad_core"][rows, :]

    def reduce_second(self):
        here = self.here
        self.core_copy.wait_recv()
        self.reduce_copies = []
        offsets = [(dyh, dz) for dyh in (1, 0) for dz in (2, 1, 3, 0)][:-1]
        for i, (dyh, dz) in enumerate(offsets):
            src, dst = self.bufs["in_grad_out"].at[i], self.bufs["in_grad_in"].at[i]
            src[...] = self.core_sum(here.zblock(dyh, dz)).astype(BF16)
            self.reduce_copies.append(self.net.send(src, dst, here.dev(dyh=dyh, dz=dz)))

    def reduce_last(self):
        value = self.core_sum(self.here.gz)
        for i, copy in enumerate(self.reduce_copies):
            copy.wait_recv()
            value = value + self.bufs["in_grad_in"][i].astype(F32)
        self.shared["in_grad"][pl.ds(self.first, self.size), :] = value.T.astype(BF16)


def chunk_scratch(size, block):
    tokens = 2 * size
    h = block // 2
    sums = {
        "out": pltpu.VMEM((2, 3, block, tokens), BF16),
        "far": pltpu.VMEM((2, 2, h, tokens), BF16),
        "near": pltpu.VMEM((2, 2, block, tokens), BF16),
    }
    return {
        "acts": pltpu.VMEM((2, 768, tokens), BF16),
        "pre": {
            "out": pltpu.VMEM((1, 3, block, tokens), BF16),
            "far": pltpu.VMEM((1, 2, h, tokens), BF16),
            "near": pltpu.VMEM((1, 2, block, tokens), BF16),
            "y_out": pltpu.VMEM((4, block, tokens), BF16),
            "y_in": pltpu.VMEM((4, block, tokens), BF16),
        },
        "back": dict(
            sums,
            y_out=pltpu.VMEM((1, block, tokens), BF16),
            y_in=pltpu.VMEM((1, block, tokens), BF16),
        ),
        "hidden": pltpu.VMEM((block, tokens), F32),
        "hidden_back": pltpu.VMEM((block, tokens), F32),
        "activation": pltpu.VMEM((8 * block, tokens), BF16),
        "pre_grad": pltpu.VMEM((8 * block, tokens), BF16),
        "in_grad": pltpu.VMEM((768, tokens), F32),
        "in_grad_core": pltpu.VMEM((768, size), F32),
        "in_grad_out": pltpu.VMEM((7, 96, size), BF16),
        "in_grad_in": pltpu.VMEM((7, 96, size), BF16),
    }


def kernel(inputs, out_grad, up_hbm, down_hbm, in_grad, up_grad, down_grad, scratch):
    here = Place()
    net = Net(scratch["send_sems"], scratch["recv_sems"])
    local_sems = scratch["local_sems"]
    shared = dict(scratch["shared"])
    shared.update(
        inputs=inputs, out_grad=out_grad, in_grad=in_grad, up_grad=up_grad, down_grad=down_grad,
        block=192, local_sems=local_sems, flushes=[],
    )
    loads = [
        pltpu.make_async_copy(up_hbm, shared["up"], local_sems.at[4]),
        pltpu.make_async_copy(down_hbm, shared["down"], local_sems.at[5]),
    ]
    for copy in loads:
        copy.start()
    chunks = [Chunk(i, net, here, scratch["chunks"][i], shared) for i in range(len(CHUNKS))]
    for chunk in chunks:
        chunk.load()

    barrier = pltpu.get_barrier_semaphore()
    partners = [here.dev(dc=1), here.dev(dyl=1), here.dev(dx=1), here.dev(dx=3)]
    partners += [here.dev(dyh=dyh, dz=dz) for dyh in range(2) for dz in range(4) if dyh or dz]
    for device in partners:
        pl.semaphore_signal(barrier, inc=1, device_id=device, device_id_type=MESH)
    pl.semaphore_wait(barrier, len(partners))

    def turn(first, count):
        @pl.loop(first, first + count)
        def _(i):
            rows = pl.ds(pl.multiple_of(i * 128, 128), 128)
            shared["up_t"][rows, :] = shared["up"][:, rows].T

    first, rest = chunks[0], chunks[1:]
    first.gather_start()
    loads[0].wait()
    turn(0, 4)
    first.gather_second()
    turn(4, 8)
    first.gather_third()
    first.gather_last()
    loads[1].wait()
    first.sum_start()
    for i, chunk in enumerate(rest):
        before = chunks[i]
        chunk.gather_start()
        before.sum_second()
        chunk.gather_second()
        chunk.gather_third()
        before.sum_third()
        chunk.gather_last()
        chunk.sum_start()
        before.activate()
        before.share_start()
        if i:
            chunks[i - 1].share_second()
            chunks[i - 1].share_third()
            chunks[i - 1].finish()
    last = chunks[-1]
    last.sum_second()
    last.sum_third()
    if rest:
        before = chunks[-2]
        before.share_second()
    last.activate()
    last.share_start()
    if rest:
        before.share_third()
        before.grad_share.own_row()
        before.in_grad_rows(here.yl, False)
        before.weight_grads(here.yl)
    last.share_second()
    if rest:
        before.grad_share.other_row()
        before.in_grad_rows(1 - here.yl, True)
        before.reduce_start()
        before.act_share.other_row()
        before.weight_grads(1 - here.yl)
        before.reduce_second()
    last.share_third()
    last.grad_share.own_row()
    last.in_grad_rows(here.yl, False)
    last.weight_grads(here.yl)
    if rest:
        before.reduce_last()
    last.grad_share.other_row()
    last.in_grad_rows(1 - here.yl, True)
    last.reduce_start()
    last.act_share.other_row()
    last.reduce_second()
    last.weight_grads(1 - here.yl)
    last.reduce_last()
    for copy in shared["flushes"]:
        copy.wait()
    net.drain()


def body(inputs, out_grad, up_weight, down_weight):
    block = 192
    scratch = {
        "send_sems": pltpu.SemaphoreType.DMA((SEMS,)),
        "recv_sems": pltpu.SemaphoreType.DMA((SEMS,)),
        "local_sems": pltpu.SemaphoreType.DMA((6,)),
        "shared": {
            "up": pltpu.VMEM((768, 1536), BF16),
            "up_t": pltpu.VMEM((1536, 768), BF16),
            "down": pltpu.VMEM((1536, 768), BF16),
            "up_total": pltpu.VMEM((768, 1536), F32),
            "down_total": pltpu.VMEM((1536, 768), F32),
            "up_stage": pltpu.VMEM((768, 1536), BF16),
            "down_stage": pltpu.VMEM((1536, 768), BF16),
        },
        "chunks": [chunk_scratch(size, block) for _, size in CHUNKS],
    }
    leaves, tree = jax.tree.flatten(scratch)

    def run(*refs):
        kernel(*refs[:7], jax.tree.unflatten(tree, refs[7:]))

    vmem, hbm = pl.BlockSpec(memory_space=pltpu.VMEM), pl.BlockSpec(memory_space=pl.ANY)
    return pl.pallas_call(
        run,
        out_shape=(
            jax.ShapeDtypeStruct((640, 96), BF16),
            jax.ShapeDtypeStruct((768, 1536), BF16),
            jax.ShapeDtypeStruct((1536, 768), BF16),
        ),
        in_specs=[vmem, vmem, hbm, hbm],
        out_specs=(vmem, hbm, hbm),
        scratch_shapes=leaves,
        compiler_params=pltpu.CompilerParams(
            collective_id=0, has_side_effects=True, vmem_limit_bytes=63 * 2**20
        ),
        cost_estimate=pl.CostEstimate(
            flops=15_100_000_000, bytes_accessed=10_000_000, transcendentals=245_760
        ),
        name="mlp_backward",
    )(inputs, out_grad, up_weight, down_weight)


def solution(mesh):
    return jax.shard_map(
        body,
        mesh=mesh,
        in_specs=(
            P("gx", ("gy", "gz")),
            P("gx", ("gy", "gz")),
            P("gy", ("gx", "gz")),
            P(("gx", "gz"), "gy"),
        ),
        out_specs=(P("gx", ("gy", "gz")), P("gy", ("gx", "gz")), P(("gx", "gz"), "gy")),
        check_vma=False,
    )
```

time: 572 us -> 173 us (0.30)
  waiting for transfers between devices: 417 us -> 0 us
  Pallas kernels: 0 us -> 162 us
  blocking collectives: 74 us -> 0 us
  matrix products: 43.7 us -> 0 us
  other arithmetic: 16.7 us -> 0 us
  between operations: 14.1 us -> 0.64 us
    psum x1 -> x0, waiting for transfers between devices: 324 us -> none  [body(): hidden_pre, act_grad = lax.psum((pre_part, back_part), 'gy')]
    pallas_call x0 -> x1, Pallas kernels: none -> 162 us  [body(): pl.pallas_call(run, out_shape=(jax.ShapeDtypeStruct((640, 96), BF16), jax...]
    reduce_scatter x3 -> x0, waiting for transfers between devices: 92 us -> none  [the longest x1 52.7 us: width_shares(): return lax.psum_scatter(partial_grad, 'gz', scatter_dimension=1, tiled=True)]
    all_gather x2 -> x0, blocking collectives: 74 us -> none  [the longest x1 37.4 us: body(): lax.all_gather(inputs, 'gz', axis=1, tiled=True)]
    dot_general x5 -> x0, matrix products: 43.7 us -> none  [the longest x4 35 us: contract_dims(): lax.dot_general(left, right, (((left_dim,), (right_dim,)), ((), ())), pre...]
    convert_element_type x4 -> x0, other arithmetic: 16.7 us -> none  [the longest x1 8.54 us: activate(): (act_grad * deriv).astype(jnp.bfloat16)]
  transfers between devices with their start and end apart: 6 -> 0, of which waited for: 4 -> 0; matrix products, arithmetic and copies ran while one was open for 6% -> 0% of each run, Pallas kernels for 0% -> 0%
where the time goes in v1:
time: 173 us; the launch traced here: 172 us
  Pallas kernels  162 us (94%)
  local copies, waits for them, and re-layouts  9.88 us (6%)
    pallas_call x1, Pallas kernels, body(): pl.pallas_call(run, out_shape=(jax.ShapeDtypeStruct((640, 96), BF16), jax...  162 us
    unnamed x6, local copies, waits for them, and re-layouts  8.19 us

profile of v1, /device:TPU:0, one launch (start us, length us, event | category | flops | bytes accessed | tf_op | source)
XLA Modules:
  0.0 172.2 jit_solution(14356324122852571690)
XLA Ops:
  0.6 1.7 copy.7.refs_0_
  2.3 1.7 copy.8.refs_1_
  4.0 161.7 %mlp_backward.1 = (bf16[640,96]{1,0:T(8,128)(2,1)}, bf16[768,1536]{1,0:T(8,128)(2,1)}, bf16[1536,768]{1,0:T(8,128)(2,1)}) custom-call(bf16[640,96]{1,0:T(8,128)(2,1)} %copy.7.refs_0_, bf16[640,96]{1,0:T(8,128)(2,1)} %copy.8.refs_1_, bf16[768,1536]{1,0:T(8,128)(2,1)} %refs_2_.1, bf16[1536,768]{1,0:T(8,128)(2,1)} %refs_3_.1), custom_call_target="tpu_custom_call" | custom-call | flops 15100000256 | bytes 10000000 | tf_op jit(solution)/shard_map/mlp_backward/pallas_call | solution.py:640
  165.7 1.7 copy.9
  167.4 0.0 copy-start
  167.4 3.4 %copy.12 = bf16[768,1536]{1,0:T(8,128)(2,1)} copy(bf16[768,1536]{1,0:T(8,128)(2,1)} %get-tuple-element.10) | data formatting | bytes 4718592
  170.8 0.0 copy-done
  170.8 1.4 copy.13
Async XLA Ops:
  167.4 3.4 %copy-start = (bf16[1536,768]{1,0:T(8,128)(2,1)S(1)}, bf16[1536,768]{1,0:T(8,128)(2,1)}, u32[]{:S(2)}) copy-start(bf16[1536,768]{1,0:T(8,128)(2,1)} %get-tuple-element.11) | copy-start | bytes 7077892

commit v2 on v1

v2 whole, which is shorter than its diff:
```python
import functools

import jax
import jax.numpy as jnp
from jax import lax
from jax.experimental import pallas as pl
from jax.experimental.pallas import tpu as pltpu
from jax.sharding import PartitionSpec as P

gelu_scale = 0.7978845608028654
cubic_term = 0.044715

MESH = pl.DeviceIdType.MESH
BF16, F32 = jnp.bfloat16, jnp.float32

CHUNKS = ((0, 128), (128, 256), (384, 256))
SUMS = (('y', 'x'), ('y', 'x'), ('y', 'x'))
SHARES = (('x', 'y'), ('x', 'y'), ('y', 'y'))
REDUCES = ('z', 'z', 'direct')
SEMS = 90 * len(CHUNKS)
BLOCK = 192
HALF = 96
WIDTH = 768
ROW = 768

PLACES = ((2, 0), (2, 1), (1, 1), (3, 0), (1, 0), (3, 1), (0, 0), (0, 1))


def nn(left, right):
    return jnp.dot(left, right, preferred_element_type=F32)


def nt(left, right):
    return lax.dot_general(left, right, (((1,), (1,)), ((), ())), preferred_element_type=F32)


def aligned(index, step):
    return pl.multiple_of(index * step, step)


class Place:
    def __init__(self):
        self.c = lax.axis_index("gx")
        self.gy = lax.axis_index("gy")
        self.gz = lax.axis_index("gz")
        self.yl, self.x = self.gy // 4, self.gy % 4
        self.yh, self.z = self.gz // 4, self.gz % 4

    def dev(self, dc=0, dyl=0, dx=0, dyh=0, dz=0):
        return (
            (self.c + dc) % 2,
            self.owner((self.yl + dyl) % 2, dx),
            self.zblock(dyh, dz),
        )

    def owner(self, row, dx):
        return row * 4 + (self.x + dx) % 4

    def zblock(self, dyh, dz):
        return ((self.yh + dyh) % 2) * 4 + (self.z + dz) % 4


class Net:
    def __init__(self, send_sems, recv_sems):
        self.send_sems, self.recv_sems = send_sems, recv_sems
        self.copies = []

    def send(self, src, dst, device):
        i = len(self.copies)
        assert i < SEMS
        copy = pltpu.make_async_remote_copy(
            src_ref=src,
            dst_ref=dst,
            send_sem=self.send_sems.at[i],
            recv_sem=self.recv_sems.at[i],
            device_id=device,
            device_id_type=MESH,
        )
        copy.start()
        self.copies.append(copy)
        return copy

    def drain(self):
        for copy in self.copies:
            copy.wait_send()


class Ring:
    def __init__(self, net, here, out, far, near):
        self.net, self.out, self.far, self.near = net, out, far, near
        self.right, self.left = here.dev(dx=1), here.dev(dx=3)

    def push(self, place, dst, device):
        return self.net.send(self.out.at[pl.ds(place * HALF, HALF)], dst, device)

    def opposite(self):
        self.far_copies = [
            self.push(0, self.far.at[0], self.right), self.push(1, self.far.at[1], self.left)
        ]

    def beside(self):
        self.near_copies = [
            self.push(2, self.near.at[0, pl.ds(HALF, HALF)], self.right),
            self.push(3, self.near.at[1, pl.ds(0, HALF)], self.left),
        ]

    def relay(self, parts):
        for i, device in enumerate((self.right, self.left)):
            part = parts(i)
            self.far_copies[i].wait_recv()
            self.out[pl.ds((4 + i) * HALF, HALF)] = (part + self.far[i].astype(F32)).astype(BF16)
            self.near_copies.append(
                self.push(4 + i, self.near.at[i, pl.ds(i * HALF, HALF)], device)
            )

    def arrive(self):
        for copy in self.near_copies:
            copy.wait_recv()

    def add(self, part, half):
        rows = pl.ds(half * HALF, HALF)
        return part + self.near[0, rows].astype(F32) + self.near[1, rows].astype(F32)


class YFirst:
    def __init__(self, net, here, bufs, weight, acts):
        self.net, self.here, self.bufs = net, here, bufs
        self.weight, self.acts = weight, acts
        self.ring = Ring(net, here, bufs["out"].at[0], bufs["far"].at[0], bufs["near"].at[0])

    def start(self):
        y_out, y_in = self.bufs["y_out"], self.bufs["y_in"]
        self.y_copies = []
        for i in range(2):
            rows = pl.ds(i * 2 * BLOCK, 2 * BLOCK)
            y_out[rows] = nn(self.weight[rows], self.acts[...]).astype(BF16)
            for j in (2 * i, 2 * i + 1):
                rows = pl.ds(j * BLOCK, BLOCK)
                self.y_copies.append(self.net.send(y_out.at[rows], y_in.at[rows], self.here.dev(dyl=1)))

    def rest(self):
        for i in range(2):
            rows, weight_rows = pl.ds(i * 2 * BLOCK, 2 * BLOCK), pl.ds(ROW + i * 2 * BLOCK, 2 * BLOCK)
            self.bufs["held"][rows] = nn(self.weight[weight_rows], self.acts[...])

    def part(self, place):
        rows = pl.ds(place * HALF, HALF)
        return self.bufs["held"][rows] + self.bufs["y_in"][rows].astype(F32)

    def fill(self, i):
        self.y_copies[i].wait_recv()
        for place in (2 * i, 2 * i + 1):
            self.ring.out[pl.ds(place * HALF, HALF)] = self.part(place).astype(BF16)

    def first(self):
        self.fill(0)
        self.ring.opposite()

    def second(self):
        self.fill(1)
        self.ring.beside()

    def third(self):
        self.y_copies[2].wait_recv()
        self.ring.relay(lambda i: self.part(4 + i))

    def last(self):
        self.y_copies[3].wait_recv()
        self.ring.arrive()

    def total(self, half):
        return self.ring.add(self.part(6 + half), half)


class XFirst:
    def __init__(self, net, here, bufs, weight, acts):
        self.net, self.here, self.bufs = net, here, bufs
        self.weight, self.acts = weight, acts
        self.rings = [
            Ring(net, here, bufs["out"].at[i], bufs["far"].at[i], bufs["near"].at[i]) for i in range(2)
        ]

    def start(self):
        for i, ring in enumerate(self.rings):
            ring.out[pl.ds(0, 2 * BLOCK)] = nn(
                self.weight[pl.ds(i * ROW, 2 * BLOCK)], self.acts[...]
            ).astype(BF16)
            ring.opposite()
        for ring in self.rings:
            ring.beside()

    def rest(self):
        for i in range(2):
            self.bufs["held"][pl.ds(i * 2 * BLOCK, 2 * BLOCK)] = nn(
                self.weight[pl.ds(i * ROW + 2 * BLOCK, 2 * BLOCK)], self.acts[...]
            )

    def part(self, ring, place):
        return self.bufs["held"][pl.ds(ring * 2 * BLOCK + (place - 4) * HALF, HALF)]

    def first(self):
        self.rings[0].relay(lambda i: self.part(0, 4 + i))

    def second(self):
        self.rings[1].relay(lambda i: self.part(1, 4 + i))

    def third(self):
        self.rings[0].arrive()
        y_out, y_in = self.bufs["y_out"].at[pl.ds(0, BLOCK)], self.bufs["y_in"].at[pl.ds(0, BLOCK)]
        for half in range(2):
            y_out[pl.ds(half * HALF, HALF)] = self.rings[0].add(self.part(0, 6 + half), half).astype(BF16)
        self.y_copy = self.net.send(y_out, y_in, self.here.dev(dyl=1))

    def last(self):
        self.rings[1].arrive()
        self.y_copy.wait_recv()

    def total(self, half):
        rows = pl.ds(half * HALF, HALF)
        return self.rings[1].add(self.part(1, 6 + half), half) + self.bufs["y_in"][rows].astype(F32)


class Share:
    def __init__(self, net, here, buf, row, block):
        self.net, self.here, self.buf, self.row, self.block = net, here, buf, row, block
        self.h = block // 2
        self.right, self.left = here.dev(dx=1), here.dev(dx=3)

    def ref(self, dx, half=None):
        owner = self.here.owner(self.row, dx)
        if half is None:
            return self.buf.at[pl.ds(aligned(owner, self.block), self.block)]
        return self.buf.at[pl.ds(aligned(owner * 2 + half, self.h), self.h)]

    def push(self, ref, device):
        return self.net.send(ref, ref, device)

    def start(self):
        first = [self.push(self.ref(0, 0), self.right), self.push(self.ref(0, 1), self.left)]
        second = [self.push(self.ref(0, 1), self.right), self.push(self.ref(0, 0), self.left)]
        self.first, self.second = first, second

    def relay(self):
        self.first[0].wait_recv()
        self.far = [self.push(self.ref(3, 0), self.right)]
        self.first[1].wait_recv()
        self.far.append(self.push(self.ref(1, 1), self.left))

    def arrive_near(self):
        for copy in self.second:
            copy.wait_recv()

    def arrive_far(self):
        for copy in self.far:
            copy.wait_recv()


class ShareXFirst:
    def __init__(self, net, here, buf, block):
        self.net, self.here = net, here
        self.ring = Share(net, here, buf, here.yl, block)

    def over(self, dx):
        ref = self.ring.ref(dx)
        self.y_copies.append(self.net.send(ref, ref, self.here.dev(dyl=1)))

    def start(self):
        self.y_copies = []
        self.ring.start()
        self.over(0)

    def first(self):
        self.ring.relay()

    def second(self):
        self.ring.arrive_near()
        self.over(1)
        self.over(3)

    def third(self):
        self.ring.arrive_far()
        self.over(2)

    def own_row(self):
        pass

    def other_row(self):
        for copy in self.y_copies:
            copy.wait_recv()


class ShareYFirst:
    def __init__(self, net, here, buf, block):
        self.net, self.here = net, here
        self.rings = [Share(net, here, buf, row, block) for row in (here.yl, 1 - here.yl)]

    def start(self):
        ref = self.rings[0].ref(0)
        self.y_copy = self.net.send(ref, ref, self.here.dev(dyl=1))
        self.rings[0].start()

    def first(self):
        self.rings[0].relay()

    def second(self):
        self.y_copy.wait_recv()
        self.rings[1].start()

    def third(self):
        self.rings[1].relay()

    def own_row(self):
        self.rings[0].arrive_near()
        self.rings[0].arrive_far()

    def other_row(self):
        self.rings[1].arrive_near()
        self.rings[1].arrive_far()


class Chunk:
    def __init__(self, index, net, here, bufs, shared):
        self.first, self.size = CHUNKS[index]
        self.index = index
        self.is_first, self.is_last = index == 0, index == len(CHUNKS) - 1
        self.net, self.here, self.bufs, self.shared = net, here, bufs, shared

    def run(self, step):
        name, _, part = step.rpartition("_")
        if name in ("pre", "back", "act", "grad"):
            getattr(getattr(self, name), part)()
        else:
            getattr(self, step)()

    def feature_ref(self, zblock, core):
        return self.bufs["acts"].at[
            :, pl.ds(aligned(zblock, HALF), HALF), pl.ds(aligned(core, self.size), self.size)
        ]

    def pass_on(self, zblock, device):
        ref = self.feature_ref(zblock, self.here.c)
        return self.net.send(ref, ref, device)

    def load(self):
        here = self.here
        rows = pl.ds(aligned(here.gz, HALF), HALF)
        lanes = pl.ds(aligned(here.c, self.size), self.size)
        self.loads = []
        for i, name in enumerate(("inputs", "out_grad")):
            self.loads.append(
                self.shared["fetch"](
                    self.shared[name].at[:, pl.ds(self.first, self.size)],
                    self.bufs["acts"].at[i, rows, lanes],
                )
            )

    def gather_start(self):
        here = self.here
        for copy in self.loads:
            copy.wait()
        self.y_copy = self.pass_on(here.gz, here.dev(dyh=1))
        self.z_copies = [self.pass_on(here.gz, here.dev(dz=dz)) for dz in (1, 3, 2)]
        self.core_copies = [self.pass_on(here.gz, here.dev(dc=1))]

    def gather_second(self):
        here = self.here
        self.y_copy.wait_recv()
        block = here.zblock(1, 0)
        self.z_copies += [self.pass_on(block, here.dev(dz=dz)) for dz in (1, 3, 2)]
        self.core_copies.append(self.pass_on(block, here.dev(dc=1)))

    def gather_third(self):
        here = self.here
        for i in range(3):
            self.z_copies[i].wait_recv()
            self.core_copies.append(self.pass_on(here.zblock(0, (3, 1, 2)[i]), here.dev(dc=1)))

    def gather_fourth(self):
        here = self.here
        for i in range(3):
            self.z_copies[3 + i].wait_recv()
            self.core_copies.append(self.pass_on(here.zblock(1, (3, 1, 2)[i]), here.dev(dc=1)))

    def gather_last(self):
        for copy in self.core_copies:
            copy.wait_recv()

    def sum_start(self):
        acts = self.bufs["acts"]
        kinds = {"y": YFirst, "x": XFirst}
        sums = []
        for i, (name, weight) in enumerate((("pre", "up_t"), ("back", "down"))):
            kind = kinds[SUMS[self.index][i]]
            sums.append(kind(self.net, self.here, self.bufs[name], self.shared[weight], acts.at[i]))
        self.pre, self.back = sums
        self.back.start()
        self.pre.start()
        self.back.rest()
        self.pre.rest()

    def activate(self):
        self.back.last()
        self.pre.last()
        hidden, back = self.bufs["pre"]["held"], self.bufs["back"]["held"]
        at = 6 * HALF
        for half in range(2):
            rows = pl.ds(at + half * HALF, HALF)
            hidden[rows] = self.pre.total(half)
            back[rows] = self.back.total(half)
        base = self.here.gy * BLOCK

        @pl.loop(0, BLOCK // 16)
        def _(i):
            rows = pl.ds(pl.multiple_of(at + i * 16, 16), 16)
            to = pl.ds(pl.multiple_of(base + i * 16, 16), 16)
            x = hidden[rows, :]
            t = jnp.tanh(gelu_scale * (x + cubic_term * x * x * x))
            deriv = 0.5 * (1.0 + t) + 0.5 * x * (1.0 - t * t) * gelu_scale * (1.0 + 3.0 * cubic_term * x * x)
            self.bufs["activation"][to, :] = (0.5 * x * (1.0 + t)).astype(BF16)
            self.bufs["pre_grad"][to, :] = (back[rows, :] * deriv).astype(BF16)

        self.share_start()

    def share_start(self):
        kinds = {"x": ShareXFirst, "y": ShareYFirst}
        act, grad = SHARES[self.index]
        self.act_share = kinds[act](self.net, self.here, self.bufs["activation"], BLOCK)
        self.grad_share = kinds[grad](self.net, self.here, self.bufs["pre_grad"], BLOCK)
        self.grad, self.act = self.grad_share, self.act_share
        self.grad.start()
        self.act.start()

    def in_grad_rows(self, row, add):
        up, pre_grad, total = self.shared["up"], self.bufs["pre_grad"], self.bufs["in_grad"]
        cols = pl.ds(aligned(row, ROW), ROW)

        @pl.loop(0, 2)
        def _(i):
            rows = pl.ds(pl.multiple_of(i * 384, 384), 384)
            value = nn(up[rows, cols], pre_grad[cols, :])
            total[rows, :] = total[rows, :] + value if add else value

    def put(self, name, rows, cols, value):
        if not self.is_first:
            value = value + self.shared[name + "_total"][rows, cols]
        if self.is_last:
            self.shared[name + "_stage"][rows, cols] = value.astype(BF16)
        else:
            self.shared[name + "_total"][rows, cols] = value

    def up_rows(self, row):
        acts, pre_grad = self.bufs["acts"], self.bufs["pre_grad"]
        cols = pl.ds(aligned(row, ROW), ROW)

        @pl.loop(0, 2)
        def _(i):
            rows = pl.ds(pl.multiple_of(i * 384, 384), 384)
            self.put("up", rows, cols, nt(acts[0, rows, :], pre_grad[cols, :]))

        if self.is_last:
            part = (slice(None), cols)
            self.shared["flushes"].append(
                self.shared["fetch"](self.shared["up_stage"].at[part], self.shared["up_grad"].at[part])
            )

    def down_rows(self, row):
        acts, activation = self.bufs["acts"], self.bufs["activation"]

        @pl.loop(0, 2)
        def _(i):
            rows = pl.ds(pl.multiple_of(row * ROW + i * 384, 384), 384)
            self.put("down", rows, slice(None), nt(activation[rows, :], acts[1]))

        if self.is_last:
            part = pl.ds(aligned(row, ROW), ROW)
            self.shared["flushes"].append(
                self.shared["fetch"](self.shared["down_stage"].at[part], self.shared["down_grad"].at[part])
            )

    def in_grad_own(self):
        self.grad_share.own_row()
        self.in_grad_rows(self.here.yl, False)

    def in_grad_other(self):
        self.grad_share.other_row()
        self.in_grad_rows(1 - self.here.yl, True)
        self.reduce_start()

    def up_own(self):
        self.up_rows(self.here.yl)

    def up_other(self):
        self.up_rows(1 - self.here.yl)

    def down_own(self):
        self.act_share.own_row()
        self.down_rows(self.here.yl)

    def down_other(self):
        self.act_share.other_row()
        self.down_rows(1 - self.here.yl)

    def reduce_start(self):
        here = self.here
        theirs = pl.ds(aligned(1 - here.c, self.size), self.size)
        self.core_copy = self.net.send(
            self.bufs["in_grad"].at[:, theirs], self.bufs["in_grad_core"], here.dev(dc=1)
        )

    def core_sum(self, zblock):
        rows = pl.ds(aligned(zblock, HALF), HALF)
        mine = pl.ds(aligned(self.here.c, self.size), self.size)
        return self.bufs["in_grad"][rows, mine] + self.bufs["in_grad_core"][rows, :]

    def reduce_second(self):
        here = self.here
        self.core_copy.wait_recv()
        self.reduce_copies = []
        if REDUCES[self.index] == "direct":
            offsets = [(dyh, dz) for dyh in (1, 0) for dz in (2, 1, 3, 0)][:-1]
        else:
            offsets = [(dyh, dz) for dz in (2, 1, 3) for dyh in (1, 0)]
        for i, (dyh, dz) in enumerate(offsets):
            src, dst = self.bufs["in_grad_out"].at[i], self.bufs["in_grad_in"].at[i]
            src[...] = self.core_sum(here.zblock(dyh, dz)).astype(BF16)
            to = here.dev(dyh=dyh, dz=dz) if REDUCES[self.index] == "direct" else here.dev(dz=dz)
            self.reduce_copies.append(self.net.send(src, dst, to))

    def gathered(self, zblock, indices):
        value = self.core_sum(zblock)
        for i in indices:
            self.reduce_copies[i].wait_recv()
            value = value + self.bufs["in_grad_in"][i].astype(F32)
        return value

    def reduce_third(self):
        if REDUCES[self.index] == "direct":
            return
        src, dst = self.bufs["in_grad_out"].at[6], self.bufs["in_grad_in"].at[6]
        src[...] = self.gathered(self.here.zblock(1, 0), (0, 2, 4)).astype(BF16)
        self.reduce_copies.append(self.net.send(src, dst, self.here.dev(dyh=1)))

    def reduce_last(self):
        indices = range(7) if REDUCES[self.index] == "direct" else (1, 3, 5, 6)
        value = self.gathered(self.here.gz, indices)
        self.shared["in_grad"][:, pl.ds(self.first, self.size)] = value.astype(BF16)


ORDER = (
    "0.gather_start", "0.gather_second", "0.gather_third", "1.gather_start", "0.gather_fourth", "1.gather_second",
    "0.gather_last", "0.sum_start", "0.back_first", "1.gather_fourth", "1.gather_third", "2.gather_start",
    "0.back_second", "0.back_third", "1.gather_last", "1.sum_start", "0.pre_first", "1.back_first", "2.gather_third",
    "0.pre_second", "0.pre_third", "1.back_second", "2.gather_second", "0.activate", "2.gather_fourth",
    "2.gather_last", "2.sum_start", "0.act_first", "2.back_first", "1.pre_first", "2.back_second", "1.pre_second",
    "0.grad_second", "0.grad_first", "0.grad_third", "1.pre_third", "0.in_grad_own", "1.back_third", "2.pre_first",
    "2.pre_second", "1.activate", "0.in_grad_other", "2.pre_third", "0.reduce_second", "0.up_other", "0.reduce_third",
    "2.back_third", "1.grad_second", "1.grad_first", "1.act_first", "0.act_second", "2.activate", "1.grad_third",
    "0.reduce_last", "0.act_third", "1.in_grad_own", "2.grad_second", "1.act_second", "1.act_third",
    "1.in_grad_other", "2.grad_first", "0.up_own", "0.down_own", "1.up_other", "2.grad_third", "1.reduce_second",
    "1.up_own", "2.in_grad_own", "2.act_second", "2.in_grad_other", "0.down_other", "2.act_first", "1.down_own",
    "1.reduce_third", "2.reduce_second", "1.down_other", "2.act_third", "2.reduce_third", "1.reduce_last", "2.up_own",
    "2.up_other", "2.down_own", "2.down_other", "2.reduce_last",
)


def chunk_scratch(size, index):
    tokens = 2 * size

    def sums(rows, y_rows):
        return {
            "held": pltpu.VMEM((ROW, tokens), F32),
            "out": pltpu.VMEM((rows, 3 * BLOCK, tokens), BF16),
            "far": pltpu.VMEM((rows, 2, HALF, tokens), BF16),
            "near": pltpu.VMEM((rows, 2, BLOCK, tokens), BF16),
            "y_out": pltpu.VMEM((y_rows, tokens), BF16),
            "y_in": pltpu.VMEM((y_rows, tokens), BF16),
        }

    shapes = {"y": (1, ROW), "x": (2, BLOCK)}
    return {
        "acts": pltpu.VMEM((2, WIDTH, tokens), BF16),
        "pre": sums(*shapes[SUMS[index][0]]),
        "back": sums(*shapes[SUMS[index][1]]),
        "activation": pltpu.VMEM((8 * BLOCK, tokens), BF16),
        "pre_grad": pltpu.VMEM((8 * BLOCK, tokens), BF16),
        "in_grad": pltpu.VMEM((WIDTH, tokens), F32),
        "in_grad_core": pltpu.VMEM((WIDTH, size), F32),
        "in_grad_out": pltpu.VMEM((7, HALF, size), BF16),
        "in_grad_in": pltpu.VMEM((7, HALF, size), BF16),
    }


def kernel(inputs, out_grad, up_hbm, down_hbm, in_grad, up_grad, down_grad, scratch):
    here = Place()
    net = Net(scratch["send_sems"], scratch["recv_sems"])
    shared = dict(scratch["shared"])
    fetched = []

    def fetch(src, dst):
        copy = pltpu.make_async_copy(src, dst, scratch["local_sems"].at[len(fetched)])
        fetched.append(copy)
        copy.start()
        return copy

    shared.update(
        inputs=inputs, out_grad=out_grad, in_grad=in_grad, up_grad=up_grad, down_grad=down_grad,
        fetch=fetch, flushes=[],
    )
    chunks = [Chunk(i, net, here, scratch["chunks"][i], shared) for i in range(len(CHUNKS))]
    chunks[0].load()
    up_load = fetch(up_hbm, shared["up"])
    down_loads = []
    for row in range(2):
        for place, (dx, half) in enumerate(PLACES):
            first = aligned(here.owner((here.yl + 1 - row) % 2, dx) * 2 + half, HALF)
            down_loads.append(
                fetch(
                    down_hbm.at[pl.ds(first, HALF)],
                    shared["down"].at[pl.ds(row * ROW + place * HALF, HALF)],
                )
            )
    for chunk in chunks[1:]:
        chunk.load()

    natural = shared["down_stage"]

    def turn_up():
        for i in range(4):
            part = pl.ds(i * 384, 384)
            natural[part, :] = shared["up"][:, part].T

    def place_up():
        for row in range(2):
            for place, (dx, half) in enumerate(PLACES):
                source = aligned(here.owner((here.yl + 1 - row) % 2, dx) * 2 + half, HALF)
                shared["up_t"][pl.ds(row * ROW + place * HALF, HALF)] = natural[pl.ds(source, HALF)]

    barrier = pltpu.get_barrier_semaphore()
    partners = [here.dev(dc=1), here.dev(dyl=1), here.dev(dx=1), here.dev(dx=3)]
    partners += [here.dev(dyh=dyh, dz=dz) for dyh in range(2) for dz in range(4) if dyh or dz]
    for device in partners:
        pl.semaphore_signal(barrier, inc=1, device_id=device, device_id_type=MESH)
    pl.semaphore_wait(barrier, len(partners))

    for word in ORDER:
        chunk, step = chunks[int(word.split(".")[0])], word.split(".")[1]
        if word == "0.gather_second":
            up_load.wait()
            turn_up()
        if word == "0.gather_third":
            place_up()
        if word == "0.sum_start":
            for copy in down_loads:
                copy.wait()
        chunk.run(step)
    for copy in shared["flushes"]:
        copy.wait()
    net.drain()


def body(inputs, out_grad, up_weight, down_weight):
    scratch = {
        "send_sems": pltpu.SemaphoreType.DMA((SEMS,)),
        "recv_sems": pltpu.SemaphoreType.DMA((SEMS,)),
        "local_sems": pltpu.SemaphoreType.DMA((17 + 2 * len(CHUNKS) + 4,)),
        "shared": {
            "up": pltpu.VMEM((WIDTH, 2 * ROW), BF16),
            "up_t": pltpu.VMEM((2 * ROW, WIDTH), BF16),
            "down": pltpu.VMEM((2 * ROW, WIDTH), BF16),
            "up_total": pltpu.VMEM((WIDTH, 2 * ROW), F32),
            "down_total": pltpu.VMEM((2 * ROW, WIDTH), F32),
            "up_stage": pltpu.VMEM((WIDTH, 2 * ROW), BF16),
            "down_stage": pltpu.VMEM((2 * ROW, WIDTH), BF16),
        },
        "chunks": [chunk_scratch(size, i) for i, (_, size) in enumerate(CHUNKS)],
    }
    leaves, tree = jax.tree.flatten(scratch)

    def run(*refs):
        kernel(*refs[:7], jax.tree.unflatten(tree, refs[7:]))

    vmem, hbm = pl.BlockSpec(memory_space=pltpu.VMEM), pl.BlockSpec(memory_space=pl.ANY)
    in_grad, up_grad, down_grad = pl.pallas_call(
        run,
        out_shape=(
            jax.ShapeDtypeStruct((96, 640), BF16),
            jax.ShapeDtypeStruct((768, 1536), BF16),
            jax.ShapeDtypeStruct((1536, 768), BF16),
        ),
        in_specs=[hbm] * 4,
        out_specs=(vmem, hbm, hbm),
        scratch_shapes=leaves,
        compiler_params=pltpu.CompilerParams(
            collective_id=0, has_side_effects=True, vmem_limit_bytes=63 * 2**20
        ),
        cost_estimate=pl.CostEstimate(
            flops=15_100_000_000, bytes_accessed=10_000_000, transcendentals=245_760
        ),
        name="mlp_backward",
    )(inputs.T, out_grad.T, up_weight, down_weight)
    return in_grad.T, up_grad, down_grad


def solution(mesh):
    return jax.shard_map(
        body,
        mesh=mesh,
        in_specs=(
            P("gx", ("gy", "gz")),
            P("gx", ("gy", "gz")),
            P("gy", ("gx", "gz")),
            P(("gx", "gz"), "gy"),
        ),
        out_specs=(P("gx", ("gy", "gz")), P("gy", ("gx", "gz")), P(("gx", "gz"), "gy")),
        check_vma=False,
    )
```

time: 173 us -> 145 us (0.84)
  Pallas kernels: 162 us -> 137 us
  local copies, waits for them, and re-layouts: 9.88 us -> 6.34 us
    pallas_call x1, Pallas kernels: 162 us -> 137 us  [body(): pl.pallas_call(run, out_shape=(jax.ShapeDtypeStruct((96, 640), BF16), jax...]
    unnamed x6 -> x5, local copies, waits for them, and re-layouts: 8.19 us -> 6.34 us
where the time goes in v2:
time: 145 us; the launch traced here: 144 us
  Pallas kernels  137 us (94%)
  local copies, waits for them, and re-layouts  6.34 us (4%)
    pallas_call x1, Pallas kernels, body(): pl.pallas_call(run, out_shape=(jax.ShapeDtypeStruct((96, 640), BF16), jax...  137 us
    unnamed x5, local copies, waits for them, and re-layouts  6.34 us

profile of v2, /device:TPU:0, one launch (start us, length us, event | category | flops | bytes accessed | tf_op | source)
XLA Modules:
  0.0 144.5 jit_solution(2060278551993087687)
XLA Ops:
  0.6 137.5 %mlp_backward.1 = (bf16[96,640]{1,0:T(8,128)(2,1)}, bf16[768,1536]{1,0:T(8,128)(2,1)}, bf16[1536,768]{1,0:T(8,128)(2,1)}) custom-call(bf16[96,640]{1,0:T(8,128)(2,1)} %bitcast.4, bf16[96,640]{1,0:T(8,128)(2,1)} %bitcast.5, bf16[768,1536]{1,0:T(8,128)(2,1)} %refs_2_.1, bf16[1536,768]{1,0:T(8,128)(2,1)} %refs_3_.1), custom_call_target="tpu_custom_call" | custom-call | flops 15100000256 | bytes 10000000 | tf_op jit(solution)/shard_map/mlp_backward/pallas_call | solution.py:683
  138.1 1.6 %copy.10 = bf16[640,96]{0,1:T(8,128)(2,1)} copy(bf16[640,96]{0,1:T(8,128)(2,1)} %bitcast.3) | data formatting | bytes 245760
  139.7 0.0 copy-start
  139.7 3.4 %copy.11 = bf16[768,1536]{1,0:T(8,128)(2,1)} copy(bf16[768,1536]{1,0:T(8,128)(2,1)} %get-tuple-element.13) | data formatting | bytes 4718592
  143.1 0.0 copy-done
  143.1 1.4 copy.12
Async XLA Ops:
  139.7 3.4 %copy-start = (bf16[1536,768]{1,0:T(8,128)(2,1)S(1)}, bf16[1536,768]{1,0:T(8,128)(2,1)}, u32[]{:S(2)}) copy-start(bf16[1536,768]{1,0:T(8,128)(2,1)} %get-tuple-element.14) | copy-start | bytes 7077892

commit v3 on v2

v3 whole, which is shorter than its diff:
```python
import functools

import jax
import jax.numpy as jnp
from jax import lax
from jax.experimental import pallas as pl
from jax.experimental.pallas import tpu as pltpu
from jax.sharding import PartitionSpec as P

gelu_scale = 0.7978845608028654
cubic_term = 0.044715

MESH = pl.DeviceIdType.MESH
BF16, F32 = jnp.bfloat16, jnp.float32

CHUNKS = ((0, 128), (128, 256), (384, 256))
SUMS = (("y", "x"), ("y", "x"), ("y", "x"))
SHARES = (("x", "y"), ("x", "y"), ("y", "y"))
REDUCES = ("z", "z", "direct")
SEND_SEMS = 7 * len(CHUNKS)
RECV_SEMS = sum(
    19 + sum({"x": 5, "y": 7}[kind] for kind in shares) + {"direct": 1, "z": 3}[reduce]
    for shares, reduce in zip(SHARES, REDUCES)
)
BLOCK = 192
HALF = 96
WIDTH = 768
ROW = 768

PLACES = ((2, 0), (2, 1), (1, 1), (3, 0), (1, 0), (3, 1), (0, 0), (0, 1))


def nn(left, right):
    return jnp.dot(left, right, preferred_element_type=F32)


def nt(left, right):
    return lax.dot_general(left, right, (((1,), (1,)), ((), ())), preferred_element_type=F32)


def aligned(index, step):
    return pl.multiple_of(index * step, step)


class Place:
    def __init__(self):
        self.c = lax.axis_index("gx")
        self.gy = lax.axis_index("gy")
        self.gz = lax.axis_index("gz")
        self.yl, self.x = self.gy // 4, self.gy % 4
        self.yh, self.z = self.gz // 4, self.gz % 4

    def dev(self, dc=0, dyl=0, dx=0, dyh=0, dz=0):
        return (
            (self.c + dc) % 2,
            self.owner((self.yl + dyl) % 2, dx),
            self.zblock(dyh, dz),
        )

    def owner(self, row, dx):
        return row * 4 + (self.x + dx) % 4

    def zblock(self, dyh, dz):
        return ((self.yh + dyh) % 2) * 4 + (self.z + dz) % 4


class Net:
    def __init__(self, send_sems, recv_sems):
        self.send_sems, self.recv_sems = send_sems, recv_sems
        self.outboxes, self.inboxes = 0, 0

    def outbox(self):
        assert self.outboxes < SEND_SEMS
        self.outboxes += 1
        return self.outboxes - 1

    def inbox(self):
        assert self.inboxes < RECV_SEMS
        self.inboxes += 1
        return self.inboxes - 1

    def send(self, src, dst, device, outbox, inbox):
        pltpu.make_async_remote_copy(
            src_ref=src,
            dst_ref=dst,
            send_sem=self.send_sems.at[outbox],
            recv_sem=self.recv_sems.at[inbox],
            device_id=device,
            device_id_type=MESH,
        ).start()

    def arrive(self, inbox, ref):
        pltpu.make_async_copy(ref, ref, self.recv_sems.at[inbox]).wait()

    def leave(self, outbox, ref):
        pltpu.make_async_copy(ref, ref, self.send_sems.at[outbox]).wait()


class Ring:
    def __init__(self, net, here, out, far, near, outbox):
        self.net, self.out, self.far, self.near, self.outbox = net, out, far, near, outbox
        self.far_boxes, self.near_box = (net.inbox(), net.inbox()), net.inbox()
        self.right, self.left = here.dev(dx=1), here.dev(dx=3)

    def push(self, place, dst, device, inbox):
        self.net.send(self.out.at[pl.ds(place * HALF, HALF)], dst, device, self.outbox, inbox)

    def opposite(self):
        self.push(0, self.far.at[0], self.right, self.far_boxes[0])
        self.push(1, self.far.at[1], self.left, self.far_boxes[1])

    def beside(self):
        self.push(2, self.near.at[0, pl.ds(HALF, HALF)], self.right, self.near_box)
        self.push(3, self.near.at[1, pl.ds(0, HALF)], self.left, self.near_box)

    def relay(self, parts):
        for i, device in enumerate((self.right, self.left)):
            part = parts(i)
            self.net.arrive(self.far_boxes[i], self.far.at[i])
            self.out[pl.ds((4 + i) * HALF, HALF)] = (part + self.far[i].astype(F32)).astype(BF16)
            self.push(4 + i, self.near.at[i, pl.ds(i * HALF, HALF)], device, self.near_box)

    def arrive(self):
        self.net.arrive(self.near_box, self.near)

    def add(self, part, half):
        rows = pl.ds(half * HALF, HALF)
        return part + self.near[0, rows].astype(F32) + self.near[1, rows].astype(F32)


class YFirst:
    def __init__(self, net, here, bufs, weight, acts):
        self.net, self.here, self.bufs = net, here, bufs
        self.weight, self.acts = weight, acts
        self.outbox = net.outbox()
        self.ring = Ring(net, here, bufs["out"].at[0], bufs["far"].at[0], bufs["near"].at[0], self.outbox)
        self.y_boxes = [net.inbox() for _ in range(4)]

    def start(self):
        y_out, y_in = self.bufs["y_out"], self.bufs["y_in"]
        for i in range(2):
            rows = pl.ds(i * 2 * BLOCK, 2 * BLOCK)
            y_out[rows] = nn(self.weight[rows], self.acts[...]).astype(BF16)
            for j in (2 * i, 2 * i + 1):
                rows = pl.ds(j * BLOCK, BLOCK)
                self.net.send(y_out.at[rows], y_in.at[rows], self.here.dev(dyl=1), self.outbox, self.y_boxes[j])

    def y_arrive(self, j):
        self.net.arrive(self.y_boxes[j], self.bufs["y_in"].at[pl.ds(j * BLOCK, BLOCK)])

    def rest(self):
        for i in range(2):
            rows, weight_rows = pl.ds(i * 2 * BLOCK, 2 * BLOCK), pl.ds(ROW + i * 2 * BLOCK, 2 * BLOCK)
            self.bufs["held"][rows] = nn(self.weight[weight_rows], self.acts[...])

    def part(self, place):
        rows = pl.ds(place * HALF, HALF)
        return self.bufs["held"][rows] + self.bufs["y_in"][rows].astype(F32)

    def fill(self, i):
        self.y_arrive(i)
        for place in (2 * i, 2 * i + 1):
            self.ring.out[pl.ds(place * HALF, HALF)] = self.part(place).astype(BF16)

    def first(self):
        self.fill(0)
        self.ring.opposite()

    def second(self):
        self.fill(1)
        self.ring.beside()

    def third(self):
        self.y_arrive(2)
        self.ring.relay(lambda i: self.part(4 + i))

    def last(self):
        self.y_arrive(3)
        self.ring.arrive()

    def total(self, half):
        return self.ring.add(self.part(6 + half), half)


class XFirst:
    def __init__(self, net, here, bufs, weight, acts):
        self.net, self.here, self.bufs = net, here, bufs
        self.weight, self.acts = weight, acts
        self.outbox, self.y_box = net.outbox(), net.inbox()
        self.rings = [
            Ring(net, here, bufs["out"].at[i], bufs["far"].at[i], bufs["near"].at[i], self.outbox)
            for i in range(2)
        ]

    def start(self):
        for i, ring in enumerate(self.rings):
            ring.out[pl.ds(0, 2 * BLOCK)] = nn(
                self.weight[pl.ds(i * ROW, 2 * BLOCK)], self.acts[...]
            ).astype(BF16)
            ring.opposite()
        for ring in self.rings:
            ring.beside()

    def rest(self):
        for i in range(2):
            self.bufs["held"][pl.ds(i * 2 * BLOCK, 2 * BLOCK)] = nn(
                self.weight[pl.ds(i * ROW + 2 * BLOCK, 2 * BLOCK)], self.acts[...]
            )

    def part(self, ring, place):
        return self.bufs["held"][pl.ds(ring * 2 * BLOCK + (place - 4) * HALF, HALF)]

    def first(self):
        self.rings[0].relay(lambda i: self.part(0, 4 + i))

    def second(self):
        self.rings[1].relay(lambda i: self.part(1, 4 + i))

    def third(self):
        self.rings[0].arrive()
        y_out, y_in = self.bufs["y_out"].at[pl.ds(0, BLOCK)], self.bufs["y_in"].at[pl.ds(0, BLOCK)]
        for half in range(2):
            y_out[pl.ds(half * HALF, HALF)] = self.rings[0].add(self.part(0, 6 + half), half).astype(BF16)
        self.net.send(y_out, y_in, self.here.dev(dyl=1), self.outbox, self.y_box)

    def last(self):
        self.rings[1].arrive()
        self.net.arrive(self.y_box, self.bufs["y_in"].at[pl.ds(0, BLOCK)])

    def total(self, half):
        rows = pl.ds(half * HALF, HALF)
        return self.rings[1].add(self.part(1, 6 + half), half) + self.bufs["y_in"][rows].astype(F32)


class Share:
    def __init__(self, net, here, buf, row, outbox, apart):
        self.net, self.here, self.buf, self.row, self.outbox = net, here, buf, row, outbox
        self.right, self.left = here.dev(dx=1), here.dev(dx=3)
        self.first_boxes, self.near_box = (net.inbox(), net.inbox()), net.inbox()
        self.far_box = net.inbox() if apart else self.near_box

    def ref(self, dx, half=None):
        owner = self.here.owner(self.row, dx)
        if half is None:
            return self.buf.at[pl.ds(aligned(owner, BLOCK), BLOCK)]
        return self.buf.at[pl.ds(aligned(owner * 2 + half, HALF), HALF)]

    def push(self, ref, device, inbox):
        self.net.send(ref, ref, device, self.outbox, inbox)

    def start(self):
        self.push(self.ref(0, 0), self.right, self.first_boxes[0])
        self.push(self.ref(0, 1), self.left, self.first_boxes[1])
        self.push(self.ref(0, 1), self.right, self.near_box)
        self.push(self.ref(0, 0), self.left, self.near_box)

    def relay(self):
        self.net.arrive(self.first_boxes[0], self.ref(3, 0))
        self.push(self.ref(3, 0), self.right, self.far_box)
        self.net.arrive(self.first_boxes[1], self.ref(1, 1))
        self.push(self.ref(1, 1), self.left, self.far_box)

    def arrive_near(self):
        self.net.arrive(self.near_box, self.ref(1))

    def arrive_far(self):
        self.net.arrive(self.far_box, self.ref(2))

    def arrive_all(self):
        self.net.arrive(self.near_box, self.buf.at[pl.ds(0, 2 * BLOCK)])


class ShareXFirst:
    def __init__(self, net, here, buf):
        self.net, self.here, self.buf = net, here, buf
        self.outbox, self.y_box = net.outbox(), net.inbox()
        self.ring = Share(net, here, buf, here.yl, self.outbox, True)

    def over(self, dx):
        ref = self.ring.ref(dx)
        self.net.send(ref, ref, self.here.dev(dyl=1), self.outbox, self.y_box)

    def start(self):
        self.ring.start()
        self.over(0)

    def first(self):
        self.ring.relay()

    def second(self):
        self.ring.arrive_near()
        self.over(1)
        self.over(3)

    def third(self):
        self.ring.arrive_far()
        self.over(2)

    def own_row(self):
        pass

    def other_row(self):
        self.net.arrive(self.y_box, self.buf.at[pl.ds(aligned(1 - self.here.yl, ROW), ROW)])


class ShareYFirst:
    def __init__(self, net, here, buf):
        self.net, self.here = net, here
        self.outbox, self.y_box = net.outbox(), net.inbox()
        self.rings = [Share(net, here, buf, row, self.outbox, False) for row in (here.yl, 1 - here.yl)]

    def start(self):
        ref = self.rings[0].ref(0)
        self.net.send(ref, ref, self.here.dev(dyl=1), self.outbox, self.y_box)
        self.rings[0].start()

    def first(self):
        self.rings[0].relay()

    def second(self):
        self.net.arrive(self.y_box, self.rings[1].ref(0))
        self.rings[1].start()

    def third(self):
        self.rings[1].relay()

    def own_row(self):
        self.rings[0].arrive_all()

    def other_row(self):
        self.rings[1].arrive_all()


class Chunk:
    def __init__(self, index, net, here, bufs, shared):
        self.first, self.size = CHUNKS[index]
        self.index = index
        self.is_first, self.is_last = index == 0, index == len(CHUNKS) - 1
        self.net, self.here, self.bufs, self.shared = net, here, bufs, shared
        sums, shares = {"y": YFirst, "x": XFirst}, {"x": ShareXFirst, "y": ShareYFirst}
        pre, back = (sums[kind] for kind in SUMS[index])
        act, grad = (shares[kind] for kind in SHARES[index])
        acts = bufs["acts"]
        self.pre = pre(net, here, bufs["pre"], shared["up_t"], acts.at[0])
        self.back = back(net, here, bufs["back"], shared["down"], acts.at[1])
        self.act = act(net, here, bufs["activation"])
        self.grad = grad(net, here, bufs["pre_grad"])
        self.gather_out, self.core_out, self.reduce_out = (net.outbox() for _ in range(3))
        self.y_box, self.z_boxes, self.core_box = net.inbox(), (net.inbox(), net.inbox()), net.inbox()
        self.in_grad_box = net.inbox()
        self.reduce_boxes = [net.inbox() for _ in range(1 if REDUCES[index] == "direct" else 3)]

    def feature_ref(self, zblock, core):
        return self.bufs["acts"].at[
            :, pl.ds(aligned(zblock, HALF), HALF), pl.ds(aligned(core, self.size), self.size)
        ]

    def pass_on(self, zblock, device, inbox):
        ref = self.feature_ref(zblock, self.here.c)
        self.net.send(ref, ref, device, self.gather_out, inbox)

    def load(self):
        here = self.here
        rows = pl.ds(aligned(here.gz, HALF), HALF)
        lanes = pl.ds(aligned(here.c, self.size), self.size)
        self.loads = []
        for i, name in enumerate(("inputs", "out_grad")):
            self.loads.append(
                self.shared["fetch"](
                    self.shared[name].at[:, pl.ds(self.first, self.size)],
                    self.bufs["acts"].at[i, rows, lanes],
                )
            )

    def gather_start(self):
        here = self.here
        for copy in self.loads:
            copy.wait()
        self.pass_on(here.gz, here.dev(dyh=1), self.y_box)
        for dz in (1, 3, 2):
            self.pass_on(here.gz, here.dev(dz=dz), self.z_boxes[0])
        self.pass_on(here.gz, here.dev(dc=1), self.core_box)

    def gather_second(self):
        here = self.here
        block = here.zblock(1, 0)
        self.net.arrive(self.y_box, self.feature_ref(block, here.c))
        for dz in (1, 3, 2):
            self.pass_on(block, here.dev(dz=dz), self.z_boxes[1])
        self.pass_on(block, here.dev(dc=1), self.core_box)

    def gathered_row(self, dyh):
        here = self.here
        self.net.arrive(self.z_boxes[dyh], self.bufs["acts"].at[:, pl.ds(0, 3 * HALF), pl.ds(0, self.size)])
        for dz in (3, 1, 2):
            self.pass_on(here.zblock(dyh, dz), here.dev(dc=1), self.core_box)

    def gather_third(self):
        if self.is_first:
            self.shared["turn_up"]()
        self.gathered_row(0)

    def gather_fourth(self):
        self.gathered_row(1)

    def gather_last(self):
        theirs = pl.ds(aligned(1 - self.here.c, self.size), self.size)
        self.net.arrive(self.core_box, self.bufs["acts"].at[:, :, theirs])
        if self.is_first:
            for copy in self.shared["down_loads"]:
                copy.wait()

    def activate(self):
        self.back.last()
        self.pre.last()
        hidden, back = self.bufs["pre"]["held"], self.bufs["back"]["held"]
        at = 6 * HALF
        for half in range(2):
            rows = pl.ds(at + half * HALF, HALF)
            hidden[rows] = self.pre.total(half)
            back[rows] = self.back.total(half)
        base = self.here.gy * BLOCK

        @pl.loop(0, BLOCK // 16)
        def _(i):
            rows = pl.ds(pl.multiple_of(at + i * 16, 16), 16)
            to = pl.ds(pl.multiple_of(base + i * 16, 16), 16)
            x = hidden[rows, :]
            t = jnp.tanh(gelu_scale * (x + cubic_term * x * x * x))
            deriv = 0.5 * (1.0 + t) + 0.5 * x * (1.0 - t * t) * gelu_scale * (1.0 + 3.0 * cubic_term * x * x)
            self.bufs["activation"][to, :] = (0.5 * x * (1.0 + t)).astype(BF16)
            self.bufs["pre_grad"][to, :] = (back[rows, :] * deriv).astype(BF16)

    def in_grad_rows(self, row, add):
        up, pre_grad, total = self.shared["up"], self.bufs["pre_grad"], self.bufs["in_grad"]
        cols = pl.ds(aligned(row, ROW), ROW)

        @pl.loop(0, 2)
        def _(i):
            rows = pl.ds(pl.multiple_of(i * 384, 384), 384)
            value = nn(up[rows, cols], pre_grad[cols, :])
            total[rows, :] = total[rows, :] + value if add else value

    def put(self, name, rows, cols, value):
        if not self.is_first:
            value = value + self.shared[name + "_total"][rows, cols]
        if self.is_last:
            self.shared[name + "_grad"][rows, cols] = value.astype(BF16)
        else:
            self.shared[name + "_total"][rows, cols] = value

    def up_rows(self, row):
        acts, pre_grad = self.bufs["acts"], self.bufs["pre_grad"]
        cols = pl.ds(aligned(row, ROW), ROW)

        @pl.loop(0, 2)
        def _(i):
            rows = pl.ds(pl.multiple_of(i * 384, 384), 384)
            self.put("up", rows, cols, nt(acts[0, rows, :], pre_grad[cols, :]))

    def down_rows(self, row):
        acts, activation = self.bufs["acts"], self.bufs["activation"]

        @pl.loop(0, 2)
        def _(i):
            rows = pl.ds(pl.multiple_of(row * ROW + i * 384, 384), 384)
            self.put("down", rows, slice(None), nt(activation[rows, :], acts[1]))

    def in_grad_own(self):
        self.grad.own_row()
        self.in_grad_rows(self.here.yl, False)

    def in_grad_other(self):
        self.grad.other_row()
        self.in_grad_rows(1 - self.here.yl, True)
        self.reduce_start()

    def up_own(self):
        self.up_rows(self.here.yl)

    def up_other(self):
        self.up_rows(1 - self.here.yl)

    def down_own(self):
        self.act.own_row()
        self.down_rows(self.here.yl)

    def down_other(self):
        self.act.other_row()
        self.down_rows(1 - self.here.yl)

    def reduce_start(self):
        theirs = pl.ds(aligned(1 - self.here.c, self.size), self.size)
        self.net.send(
            self.bufs["in_grad"].at[:, theirs], self.bufs["in_grad_core"], self.here.dev(dc=1),
            self.core_out, self.in_grad_box,
        )

    def core_sum(self, zblock):
        rows = pl.ds(aligned(zblock, HALF), HALF)
        mine = pl.ds(aligned(self.here.c, self.size), self.size)
        return self.bufs["in_grad"][rows, mine] + self.bufs["in_grad_core"][rows, :]

    def reduce_send(self, i, value, device, inbox):
        src, dst = self.bufs["in_grad_out"].at[i], self.bufs["in_grad_in"].at[i]
        src[...] = value.astype(BF16)
        self.net.send(src, dst, device, self.reduce_out, inbox)

    def reduce_second(self):
        here = self.here
        self.net.arrive(self.in_grad_box, self.bufs["in_grad_core"])
        if REDUCES[self.index] == "direct":
            offsets = [(dyh, dz) for dyh in (1, 0) for dz in (2, 1, 3, 0)][:-1]
            for i, (dyh, dz) in enumerate(offsets):
                value = self.core_sum(here.zblock(dyh, dz))
                self.reduce_send(i, value, here.dev(dyh=dyh, dz=dz), self.reduce_boxes[0])
            return
        for i, (dyh, dz) in enumerate([(dyh, dz) for dyh in (1, 0) for dz in (2, 1, 3)]):
            value = self.core_sum(here.zblock(dyh, dz))
            self.reduce_send(i, value, here.dev(dz=dz), self.reduce_boxes[1 - dyh])

    def gathered(self, zblock, boxes):
        value = self.core_sum(zblock)
        for box, first, count in boxes:
            self.net.arrive(self.reduce_boxes[box], self.bufs["in_grad_in"].at[pl.ds(first, count)])
            for i in range(first, first + count):
                value = value + self.bufs["in_grad_in"][i].astype(F32)
        return value

    def reduce_third(self):
        if REDUCES[self.index] == "direct":
            return
        value = self.gathered(self.here.zblock(1, 0), ((0, 0, 3),))
        self.reduce_send(6, value, self.here.dev(dyh=1), self.reduce_boxes[2])

    def reduce_last(self):
        boxes = ((0, 0, 7),) if REDUCES[self.index] == "direct" else ((1, 3, 3), (2, 6, 1))
        value = self.gathered(self.here.gz, boxes)
        self.shared["in_grad"][:, pl.ds(self.first, self.size)] = value.astype(BF16)

    def drain(self):
        bufs = self.bufs
        self.net.leave(self.gather_out, bufs["acts"].at[:, pl.ds(0, 15 * HALF // 2)])
        for part in (self.pre, self.back, self.act, self.grad):
            self.net.leave(part.outbox, bufs["activation"].at[pl.ds(0, 14 * HALF)])
        self.net.leave(self.core_out, bufs["in_grad_core"])
        self.net.leave(self.reduce_out, bufs["in_grad_in"])


def order(chunks):
    a, b, c = chunks
    return (
        a.gather_start, a.gather_second, b.gather_start, a.gather_third, a.gather_fourth, b.gather_second,
        c.gather_start, a.gather_last, a.back.start, a.pre.start, a.back.rest, a.pre.rest, a.pre.first,
        b.gather_third, a.back.first, a.pre.second, a.back.second, b.gather_fourth, a.back.third, a.pre.third,
        c.gather_second, b.gather_last, b.back.start, b.pre.start, a.activate, b.back.rest, b.pre.rest, b.back.first,
        a.grad.start, c.gather_third, c.gather_fourth, c.gather_last, c.back.start, c.pre.start, b.back.second,
        b.pre.first, b.pre.second, b.back.third, c.pre.rest, c.back.rest, a.grad.first, a.grad.second, b.pre.third,
        c.pre.first, c.back.first, c.pre.second, c.back.second, c.pre.third, c.back.third, b.activate, a.grad.third,
        b.grad.start, a.act.start, c.activate, b.act.start, b.grad.second, b.grad.first, a.in_grad_own, a.act.first,
        a.in_grad_other, c.grad.start, a.reduce_second, b.grad.third, a.act.second, b.in_grad_own, a.up_other,
        c.grad.second, a.act.third, b.act.first, b.act.second, c.grad.first, a.down_own, c.grad.third, c.act.start,
        b.in_grad_other, a.reduce_third, b.up_other, a.up_own, b.act.third, b.down_own, b.up_own, b.reduce_second,
        c.in_grad_own, c.in_grad_other, c.up_other, c.act.first, c.act.second, a.down_other, a.reduce_last,
        c.reduce_second, c.act.third, c.reduce_third, b.reduce_third, b.down_other, c.up_own, c.reduce_last,
        c.down_own, b.reduce_last, c.down_other,
    )


def chunk_scratch(size, index):
    tokens = 2 * size

    def sums(rows, y_rows):
        return {
            "held": pltpu.VMEM((ROW, tokens), F32),
            "out": pltpu.VMEM((rows, 3 * BLOCK, tokens), BF16),
            "far": pltpu.VMEM((rows, 2, HALF, tokens), BF16),
            "near": pltpu.VMEM((rows, 2, BLOCK, tokens), BF16),
            "y_out": pltpu.VMEM((y_rows, tokens), BF16),
            "y_in": pltpu.VMEM((y_rows, tokens), BF16),
        }

    shapes = {"y": (1, ROW), "x": (2, BLOCK)}
    return {
        "acts": pltpu.VMEM((2, WIDTH, tokens), BF16),
        "pre": sums(*shapes[SUMS[index][0]]),
        "back": sums(*shapes[SUMS[index][1]]),
        "activation": pltpu.VMEM((8 * BLOCK, tokens), BF16),
        "pre_grad": pltpu.VMEM((8 * BLOCK, tokens), BF16),
        "in_grad": pltpu.VMEM((WIDTH, tokens), F32),
        "in_grad_core": pltpu.VMEM((WIDTH, size), F32),
        "in_grad_out": pltpu.VMEM((7, HALF, size), BF16),
        "in_grad_in": pltpu.VMEM((7, HALF, size), BF16),
    }


def kernel(inputs, out_grad, up_hbm, down_hbm, in_grad, up_grad, down_grad, scratch):
    here = Place()
    net = Net(scratch["send_sems"], scratch["recv_sems"])
    shared = dict(scratch["shared"])
    fetched = []

    def fetch(src, dst):
        copy = pltpu.make_async_copy(src, dst, scratch["local_sems"].at[len(fetched)])
        fetched.append(copy)
        copy.start()
        return copy

    shared.update(
        inputs=inputs, out_grad=out_grad, in_grad=in_grad, up_grad=up_grad, down_grad=down_grad, fetch=fetch
    )
    chunks = [Chunk(i, net, here, scratch["chunks"][i], shared) for i in range(len(CHUNKS))]
    chunks[0].load()
    up_load = fetch(up_hbm, shared["up"])
    down_loads = []
    for row in range(2):
        for place, (dx, half) in enumerate(PLACES):
            first = aligned(here.owner((here.yl + 1 - row) % 2, dx) * 2 + half, HALF)
            down_loads.append(
                fetch(
                    down_hbm.at[pl.ds(first, HALF)],
                    shared["down"].at[pl.ds(row * ROW + place * HALF, HALF)],
                )
            )
    for chunk in chunks[1:]:
        chunk.load()

    natural = down_grad

    def turn_up():
        up_load.wait()
        for i in range(4):
            part = pl.ds(i * 384, 384)
            natural[part, :] = shared["up"][:, part].T
        for row in range(2):
            for place, (dx, half) in enumerate(PLACES):
                source = aligned(here.owner((here.yl + 1 - row) % 2, dx) * 2 + half, HALF)
                shared["up_t"][pl.ds(row * ROW + place * HALF, HALF)] = natural[pl.ds(source, HALF)]

    shared.update(turn_up=turn_up, down_loads=down_loads)
    barrier = pltpu.get_barrier_semaphore()
    partners = [here.dev(dc=1), here.dev(dyl=1), here.dev(dx=1), here.dev(dx=3)]
    partners += [here.dev(dyh=dyh, dz=dz) for dyh in range(2) for dz in range(4) if dyh or dz]
    for device in partners:
        pl.semaphore_signal(barrier, inc=1, device_id=device, device_id_type=MESH)
    pl.semaphore_wait(barrier, len(partners))

    for step in order(chunks):
        step()
    for chunk in chunks:
        chunk.drain()


def hand_over(*refs):
    sources, results, sems = refs[:3], refs[3:6], refs[6]
    copies = []
    for i, (source, result) in enumerate(zip(sources, results)):
        copy = pltpu.make_async_copy(source, result, sems.at[i])
        copy.start()
        copies.append(copy)
    for copy in copies:
        copy.wait()


def body(inputs, out_grad, up_weight, down_weight):
    scratch = {
        "send_sems": pltpu.SemaphoreType.DMA((SEND_SEMS,)),
        "recv_sems": pltpu.SemaphoreType.DMA((RECV_SEMS,)),
        "local_sems": pltpu.SemaphoreType.DMA((17 + 2 * len(CHUNKS),)),
        "shared": {
            "up": pltpu.VMEM((WIDTH, 2 * ROW), BF16),
            "up_t": pltpu.VMEM((2 * ROW, WIDTH), BF16),
            "down": pltpu.VMEM((2 * ROW, WIDTH), BF16),
            "up_total": pltpu.VMEM((WIDTH, 2 * ROW), F32),
            "down_total": pltpu.VMEM((2 * ROW, WIDTH), F32),
        },
        "chunks": [chunk_scratch(size, i) for i, (_, size) in enumerate(CHUNKS)],
    }
    leaves, tree = jax.tree.flatten(scratch)

    def run(*refs):
        kernel(*refs[:7], jax.tree.unflatten(tree, refs[7:]))

    vmem, hbm = pl.BlockSpec(memory_space=pltpu.VMEM), pl.BlockSpec(memory_space=pl.ANY)
    in_grad, up_grad, down_grad = pl.pallas_call(
        run,
        out_shape=(
            pltpu.VMEM((HALF, 640), BF16),
            pltpu.VMEM((WIDTH, 2 * ROW), BF16),
            pltpu.VMEM((2 * ROW, WIDTH), BF16),
        ),
        in_specs=[hbm] * 4,
        out_specs=(vmem, vmem, vmem),
        scratch_shapes=leaves,
        compiler_params=pltpu.CompilerParams(
            collective_id=0, has_side_effects=True, vmem_limit_bytes=59 * 2**20
        ),
        cost_estimate=pl.CostEstimate(
            flops=15_100_000_000, bytes_accessed=10_000_000, transcendentals=245_760
        ),
        name="mlp_backward",
    )(inputs.T, out_grad.T, up_weight, down_weight)
    in_grad, up_grad, down_grad = pl.pallas_call(
        hand_over,
        out_shape=[jax.ShapeDtypeStruct(a.shape, a.dtype) for a in (in_grad, up_grad, down_grad)],
        in_specs=[hbm] * 3,
        out_specs=[hbm] * 3,
        scratch_shapes=[pltpu.SemaphoreType.DMA((3,))],
        compiler_params=pltpu.CompilerParams(vmem_limit_bytes=2**20),
        name="hand_over",
    )(in_grad, up_grad, down_grad)
    return in_grad.T, up_grad, down_grad


def solution(mesh):
    return jax.shard_map(
        body,
        mesh=mesh,
        in_specs=(
            P("gx", ("gy", "gz")),
            P("gx", ("gy", "gz")),
            P("gy", ("gx", "gz")),
            P(("gx", "gz"), "gy"),
        ),
        out_specs=(P("gx", ("gy", "gz")), P("gy", ("gx", "gz")), P(("gx", "gz"), "gy")),
        check_vma=False,
    )
```

time: 145 us -> 130 us (0.90)
  Pallas kernels: 137 us -> 129 us
  local copies, waits for them, and re-layouts: 6.34 us -> 0 us
    pallas_call x1 -> x2, Pallas kernels: 137 us -> 129 us  [the longest x1 127 us: body(): pl.pallas_call(run, out_shape=(pltpu.VMEM((HALF, 640), BF16), pltpu.VMEM(...]
    unnamed x5 -> x0, local copies, waits for them, and re-layouts: 6.34 us -> none
where the time goes in v3:
time: 130 us
  Pallas kernels  129 us (99%)
    pallas_call x1, Pallas kernels, body(): pl.pallas_call(run, out_shape=(pltpu.VMEM((HALF, 640), BF16), pltpu.VMEM(...  127 us

profile of v3, /device:TPU:0, one launch (start us, length us, event | category | flops | bytes accessed | tf_op | source)
XLA Modules:
  0.0 129.7 jit_solution(199698230058114310)
XLA Ops:
  0.6 126.6 %mlp_backward.1 = (bf16[96,640]{1,0:T(8,128)(2,1)S(1)}, bf16[768,1536]{1,0:T(8,128)(2,1)S(1)}, bf16[1536,768]{1,0:T(8,128)(2,1)S(1)}) custom-call(bf16[96,640]{1,0:T(8,128)(2,1)} %bitcast.3, bf16[96,640]{1,0:T(8,128)(2,1)} %bitcast.4, bf16[768,1536]{1,0:T(8,128)(2,1)} %refs_2_.1, bf16[1536,768]{1,0:T(8,128)(2,1)} %refs_3_.1), custom_call_target="tpu_custom_call" | custom-call | flops 15100000256 | bytes 10000000 | tf_op jit(solution)/shard_map/mlp_backward/pallas_call | solution.py:685
  127.3 2.3 %hand_over.1 = (bf16[96,640]{1,0:T(8,128)(2,1)}, bf16[768,1536]{1,0:T(8,128)(2,1)}, bf16[1536,768]{1,0:T(8,128)(2,1)}) custom-call(bf16[96,640]{1,0:T(8,128)(2,1)S(1)} %get-tuple-element.9.refs_0_, bf16[768,1536]{1,0:T(8,128)(2,1)S(1)} %get-tuple-element.10.refs_1_, bf16[1536,768]{1,0:T(8,128)(2,1)S(1)} %get-tuple-element.11.refs_2_), custom_call_target="tpu_custom_call" | custom-call | tf_op jit(solution)/shard_map/hand_over/pallas_call | solution.py:703

commit v4 on v3

--- a/solution.py
+++ b/solution.py
@@ -17,8 +17,8 @@
 SUMS = (("y", "x"), ("y", "x"), ("y", "x"))
 SHARES = (("x", "y"), ("x", "y"), ("y", "y"))
 REDUCES = ("z", "z", "direct")
-SEND_SEMS = 7 * len(CHUNKS)
-RECV_SEMS = sum(
+SEND_SEMS = 7 * len(CHUNKS) + 1
+RECV_SEMS = 4 + sum(
     19 + sum({"x": 5, "y": 7}[kind] for kind in shares) + {"direct": 1, "z": 3}[reduce]
     for shares, reduce in zip(SHARES, REDUCES)
 )
@@ -329,6 +329,57 @@
 
     def other_row(self):
         self.rings[1].arrive_all()
+
+
+class Gather:
+    def __init__(self, net, here, acts, size, first, count, ready):
+        self.net, self.here, self.size, self.ready = net, here, size, ready
+        self.acts = acts.at[pl.ds(first, count)]
+        self.outbox, self.y_box = net.outbox(), net.inbox()
+        self.z_boxes, self.core_box = (net.inbox(), net.inbox()), net.inbox()
+
+    def feature_ref(self, zblock):
+        rows = pl.ds(aligned(zblock, HALF), HALF)
+        return self.acts.at[:, rows, pl.ds(aligned(self.here.c, self.size), self.size)]
+
+    def pass_on(self, zblock, device, inbox):
+        ref = self.feature_ref(zblock)
+        self.net.send(ref, ref, device, self.outbox, inbox)
+
+    def start(self):
+        here = self.here
+        self.ready()
+        self.pass_on(here.gz, here.dev(dyh=1), self.y_box)
+        for dz in (1, 3, 2):
+            self.pass_on(here.gz, here.dev(dz=dz), self.z_boxes[0])
+        self.pass_on(here.gz, here.dev(dc=1), self.core_box)
+
+    def second(self):
+        here = self.here
+        block = here.zblock(1, 0)
+        self.net.arrive(self.y_box, self.feature_ref(block))
+        for dz in (1, 3, 2):
+            self.pass_on(block, here.dev(dz=dz), self.z_boxes[1])
+        self.pass_on(block, here.dev(dc=1), self.core_box)
+
+    def row(self, dyh):
+        here = self.here
+        self.net.arrive(self.z_boxes[dyh], self.acts.at[:, pl.ds(0, 3 * HALF), pl.ds(0, self.size)])
+        for dz in (3, 1, 2):
+            self.pass_on(here.zblock(dyh, dz), here.dev(dc=1), self.core_box)
+
+    def third(self):
+        self.row(0)
+
+    def fourth(self):
+        self.row(1)
+
+    def last(self):
+        theirs = pl.ds(aligned(1 - self.here.c, self.size), self.size)
+        self.net.arrive(self.core_box, self.acts.at[:, :, theirs])
+
+    def drain(self):
+        self.net.leave(self.outbox, self.acts.at[:, pl.ds(0, 15 * HALF // 2)])
 
 
 class Chunk:
@@ -345,19 +396,18 @@
         self.back = back(net, here, bufs["back"], shared["down"], acts.at[1])
         self.act = act(net, here, bufs["activation"])
         self.grad = grad(net, here, bufs["pre_grad"])
-        self.gather_out, self.core_out, self.reduce_out = (net.outbox() for _ in range(3))
-        self.y_box, self.z_boxes, self.core_box = net.inbox(), (net.inbox(), net.inbox()), net.inbox()
+        if self.is_first:
+            self.feat = Gather(net, here, acts, self.size, 1, 1, self.ready)
+            self.feat_two = Gather(net, here, acts, self.size, 0, 1, lambda: None)
+        else:
+            self.feat = self.feat_two = Gather(net, here, acts, self.size, 0, 2, self.ready)
+        self.core_out, self.reduce_out = net.outbox(), net.outbox()
         self.in_grad_box = net.inbox()
         self.reduce_boxes = [net.inbox() for _ in range(1 if REDUCES[index] == "direct" else 3)]
 
-    def feature_ref(self, zblock, core):
-        return self.bufs["acts"].at[
-            :, pl.ds(aligned(zblock, HALF), HALF), pl.ds(aligned(core, self.size), self.size)
-        ]
-
-    def pass_on(self, zblock, device, inbox):
-        ref = self.feature_ref(zblock, self.here.c)
-        self.net.send(ref, ref, device, self.gather_out, inbox)
+    def ready(self):
+        for copy in self.loads:
+            copy.wait()
 
     def load(self):
         here = self.here
@@ -372,44 +422,6 @@
                 )
             )
 
-    def gather_start(self):
-        here = self.here
-        for copy in self.loads:
-            copy.wait()
-        self.pass_on(here.gz, here.dev(dyh=1), self.y_box)
-        for dz in (1, 3, 2):
-            self.pass_on(here.gz, here.dev(dz=dz), self.z_boxes[0])
-        self.pass_on(here.gz, here.dev(dc=1), self.core_box)
-
-    def gather_second(self):
-        here = self.here
-        block = here.zblock(1, 0)
-        self.net.arrive(self.y_box, self.feature_ref(block, here.c))
-        for dz in (1, 3, 2):
-            self.pass_on(block, here.dev(dz=dz), self.z_boxes[1])
-        self.pass_on(block, here.dev(dc=1), self.core_box)
-
-    def gathered_row(self, dyh):
-        here = self.here
-        self.net.arrive(self.z_boxes[dyh], self.bufs["acts"].at[:, pl.ds(0, 3 * HALF), pl.ds(0, self.size)])
-        for dz in (3, 1, 2):
-            self.pass_on(here.zblock(dyh, dz), here.dev(dc=1), self.core_box)
-
-    def gather_third(self):
-        if self.is_first:
-            self.shared["turn_up"]()
-        self.gathered_row(0)
-
-    def gather_fourth(self):
-        self.gathered_row(1)
-
-    def gather_last(self):
-        theirs = pl.ds(aligned(1 - self.here.c, self.size), self.size)
-        self.net.arrive(self.core_box, self.bufs["acts"].at[:, :, theirs])
-        if self.is_first:
-            for copy in self.shared["down_loads"]:
-                copy.wait()
-
     def activate(self):
         self.back.last()
         self.pre.last()
@@ -465,6 +477,11 @@
         def _(i):
             rows = pl.ds(pl.multiple_of(row * ROW + i * 384, 384), 384)
             self.put("down", rows, slice(None), nt(activation[rows, :], acts[1]))
+
+    def prepare(self):
+        if self.is_first:
+            self.shared["turn_up"]()
+            self.shared["turn_down"]()
 
     def in_grad_own(self):
         self.grad.own_row()
@@ -540,7 +557,9 @@
 
     def drain(self):
         bufs = self.bufs
-        self.net.leave(self.gather_out, bufs["acts"].at[:, pl.ds(0, 15 * HALF // 2)])
+        self.feat.drain()
+        if self.is_first:
+            self.feat_two.drain()
         for part in (self.pre, self.back, self.act, self.grad):
             self.net.leave(part.outbox, bufs["activation"].at[pl.ds(0, 14 * HALF)])
         self.net.leave(self.core_out, bufs["in_grad_core"])
@@ -550,20 +569,20 @@
 def order(chunks):
     a, b, c = chunks
     return (
-        a.gather_start, a.gather_second, b.gather_start, a.gather_third, a.gather_fourth, b.gather_second,
-        c.gather_start, a.gather_last, a.back.start, a.pre.start, a.back.rest, a.pre.rest, a.pre.first,
-        b.gather_third, a.back.first, a.pre.second, a.back.second, b.gather_fourth, a.back.third, a.pre.third,
-        c.gather_second, b.gather_last, b.back.start, b.pre.start, a.activate, b.back.rest, b.pre.rest, b.back.first,
-        a.grad.start, c.gather_third, c.gather_fourth, c.gather_last, c.back.start, c.pre.start, b.back.second,
-        b.pre.first, b.pre.second, b.back.third, c.pre.rest, c.back.rest, a.grad.first, a.grad.second, b.pre.third,
-        c.pre.first, c.back.first, c.pre.second, c.back.second, c.pre.third, c.back.third, b.activate, a.grad.third,
-        b.grad.start, a.act.start, c.activate, b.act.start, b.grad.second, b.grad.first, a.in_grad_own, a.act.first,
-        a.in_grad_other, c.grad.start, a.reduce_second, b.grad.third, a.act.second, b.in_grad_own, a.up_other,
-        c.grad.second, a.act.third, b.act.first, b.act.second, c.grad.first, a.down_own, c.grad.third, c.act.start,
-        b.in_grad_other, a.reduce_third, b.up_other, a.up_own, b.act.third, b.down_own, b.up_own, b.reduce_second,
-        c.in_grad_own, c.in_grad_other, c.up_other, c.act.first, c.act.second, a.down_other, a.reduce_last,
-        c.reduce_second, c.act.third, c.reduce_third, b.reduce_third, b.down_other, c.up_own, c.reduce_last,
-        c.down_own, b.reduce_last, c.down_other,
+        a.feat.start, a.feat_two.start, a.feat.second, a.feat_two.second, b.feat.start, a.feat.third, a.prepare,
+        a.feat.fourth, a.feat_two.fourth, a.feat_two.third, a.feat.last, b.feat.second, c.feat.start, a.back.start,
+        a.feat_two.last, a.pre.start, a.back.rest, b.feat.third, a.back.first, a.pre.rest, a.back.second, a.pre.first,
+        b.feat.fourth, c.feat.second, a.pre.second, a.back.third, b.feat.last, b.back.start, b.pre.start,
+        c.feat.fourth, b.back.rest, c.feat.third, a.pre.third, b.back.first, b.back.second, a.activate, b.pre.rest,
+        a.grad.start, b.pre.second, b.back.third, c.feat.last, c.back.start, c.back.rest, a.grad.first, b.pre.first,
+        a.grad.second, a.act.start, c.back.second, c.pre.start, c.pre.rest, a.grad.third, a.in_grad_own, b.pre.third,
+        c.pre.second, c.pre.first, a.act.first, a.in_grad_other, b.activate, c.back.first, b.grad.start, a.act.second,
+        c.back.third, c.pre.third, b.act.start, b.grad.second, a.reduce_second, b.grad.first, a.act.third, a.down_own,
+        a.reduce_third, c.activate, b.grad.third, a.up_own, b.act.first, a.up_other, c.grad.start, b.act.second,
+        b.in_grad_own, b.in_grad_other, a.down_other, a.reduce_last, c.grad.second, b.reduce_second, b.up_other,
+        c.grad.first, c.grad.third, b.reduce_third, c.act.start, b.up_own, c.in_grad_own, b.reduce_last, b.act.third,
+        c.in_grad_other, c.act.first, b.down_own, c.act.second, c.reduce_second, c.reduce_third, c.up_other, c.up_own,
+        c.act.third, b.down_other, c.down_own, c.reduce_last, c.down_other,
     )
 
 
@@ -627,6 +646,10 @@
 
     natural = down_grad
 
+    def turn_down():
+        for copy in down_loads:
+            copy.wait()
+
     def turn_up():
         up_load.wait()
         for i in range(4):
@@ -637,7 +660,7 @@
                 source = aligned(here.owner((here.yl + 1 - row) % 2, dx) * 2 + half, HALF)
                 shared["up_t"][pl.ds(row * ROW + place * HALF, HALF)] = natural[pl.ds(source, HALF)]
 
-    shared.update(turn_up=turn_up, down_loads=down_loads)
+    shared.update(turn_up=turn_up, turn_down=turn_down)
     barrier = pltpu.get_barrier_semaphore()
     partners = [here.dev(dc=1), here.dev(dyl=1), here.dev(dx=1), here.dev(dx=3)]
     partners += [here.dev(dyh=dyh, dz=dz) for dyh in range(2) for dz in range(4) if dyh or dz]

time: 130 us -> 127 us (0.977)
  Pallas kernels: 129 us -> 126 us
    pallas_call x1, Pallas kernels: 127 us -> 124 us  [body(): pl.pallas_call(run, out_shape=(pltpu.VMEM((HALF, 640), BF16), pltpu.VMEM(...]
where the time goes in v4:
time: 127 us
  Pallas kernels  126 us (99%)
    pallas_call x1, Pallas kernels, body(): pl.pallas_call(run, out_shape=(pltpu.VMEM((HALF, 640), BF16), pltpu.VMEM(...  124 us

profile of v4, /device:TPU:0, one launch (start us, length us, event | category | flops | bytes accessed | tf_op | source)
XLA Modules:
  0.0 126.7 jit_solution(14843229229303566351)
XLA Ops:
  0.6 123.7 %mlp_backward.1 = (bf16[96,640]{1,0:T(8,128)(2,1)S(1)}, bf16[768,1536]{1,0:T(8,128)(2,1)S(1)}, bf16[1536,768]{1,0:T(8,128)(2,1)S(1)}) custom-call(bf16[96,640]{1,0:T(8,128)(2,1)} %bitcast.3, bf16[96,640]{1,0:T(8,128)(2,1)} %bitcast.4, bf16[768,1536]{1,0:T(8,128)(2,1)} %refs_2_.1, bf16[1536,768]{1,0:T(8,128)(2,1)} %refs_3_.1), custom_call_target="tpu_custom_call" | custom-call | flops 15100000256 | bytes 10000000 | tf_op jit(solution)/shard_map/mlp_backward/pallas_call | solution.py:708
  124.3 2.3 %hand_over.1 = (bf16[96,640]{1,0:T(8,128)(2,1)}, bf16[768,1536]{1,0:T(8,128)(2,1)}, bf16[1536,768]{1,0:T(8,128)(2,1)}) custom-call(bf16[96,640]{1,0:T(8,128)(2,1)S(1)} %get-tuple-element.9.refs_0_, bf16[768,1536]{1,0:T(8,128)(2,1)S(1)} %get-tuple-element.10.refs_1_, bf16[1536,768]{1,0:T(8,128)(2,1)S(1)} %get-tuple-element.11.refs_2_), custom_call_target="tpu_custom_call" | custom-call | tf_op jit(solution)/shard_map/hand_over/pallas_call | solution.py:726

commit v5 on v4

--- a/solution.py
+++ b/solution.py
@@ -332,8 +332,9 @@
 
 
 class Gather:
-    def __init__(self, net, here, acts, size, first, count, ready):
+    def __init__(self, net, here, acts, size, first, count, ready, source=None, after=None):
         self.net, self.here, self.size, self.ready = net, here, size, ready
+        self.source, self.after = source, after
         self.acts = acts.at[pl.ds(first, count)]
         self.outbox, self.y_box = net.outbox(), net.inbox()
         self.z_boxes, self.core_box = (net.inbox(), net.inbox()), net.inbox()
@@ -342,17 +343,23 @@
         rows = pl.ds(aligned(zblock, HALF), HALF)
         return self.acts.at[:, rows, pl.ds(aligned(self.here.c, self.size), self.size)]
 
-    def pass_on(self, zblock, device, inbox):
+    def pass_on(self, zblock, device, inbox, source=None):
         ref = self.feature_ref(zblock)
-        self.net.send(ref, ref, device, self.outbox, inbox)
+        if source is None:
+            self.net.send(ref, ref, device, self.outbox, inbox)
+        else:
+            self.net.send(source, ref.at[0], device, self.outbox, inbox)
 
     def start(self):
         here = self.here
-        self.ready()
-        self.pass_on(here.gz, here.dev(dyh=1), self.y_box)
+        if self.source is None:
+            self.ready()
+        self.pass_on(here.gz, here.dev(dyh=1), self.y_box, self.source)
         for dz in (1, 3, 2):
-            self.pass_on(here.gz, here.dev(dz=dz), self.z_boxes[0])
-        self.pass_on(here.gz, here.dev(dc=1), self.core_box)
+            self.pass_on(here.gz, here.dev(dz=dz), self.z_boxes[0], self.source)
+        self.pass_on(here.gz, here.dev(dc=1), self.core_box, self.source)
+        if self.after is not None:
+            self.after()
 
     def second(self):
         here = self.here
@@ -377,6 +384,8 @@
     def last(self):
         theirs = pl.ds(aligned(1 - self.here.c, self.size), self.size)
         self.net.arrive(self.core_box, self.acts.at[:, :, theirs])
+        if self.source is not None:
+            self.ready()
 
     def drain(self):
         self.net.leave(self.outbox, self.acts.at[:, pl.ds(0, 15 * HALF // 2)])
@@ -397,8 +406,14 @@
         self.act = act(net, here, bufs["activation"])
         self.grad = grad(net, here, bufs["pre_grad"])
         if self.is_first:
-            self.feat = Gather(net, here, acts, self.size, 1, 1, self.ready)
-            self.feat_two = Gather(net, here, acts, self.size, 0, 1, lambda: None)
+            columns = pl.ds(self.first, self.size)
+            self.feat = Gather(
+                net, here, acts, self.size, 1, 1, lambda: self.loads[1].wait(), shared["out_grad"].at[:, columns]
+            )
+            self.feat_two = Gather(
+                net, here, acts, self.size, 0, 1, lambda: self.loads[0].wait(), shared["inputs"].at[:, columns],
+                shared["load_rest"],
+            )
         else:
             self.feat = self.feat_two = Gather(net, here, acts, self.size, 0, 2, self.ready)
         self.core_out, self.reduce_out = net.outbox(), net.outbox()
@@ -628,22 +643,30 @@
     shared.update(
         inputs=inputs, out_grad=out_grad, in_grad=in_grad, up_grad=up_grad, down_grad=down_grad, fetch=fetch
     )
+    barrier = pltpu.get_barrier_semaphore()
+    partners = [here.dev(dc=1), here.dev(dyl=1), here.dev(dx=1), here.dev(dx=3)]
+    partners += [here.dev(dyh=dyh, dz=dz) for dyh in range(2) for dz in range(4) if dyh or dz]
+    for device in partners:
+        pl.semaphore_signal(barrier, inc=1, device_id=device, device_id_type=MESH)
+
+    up_loads, down_loads = [], []
+
+    def load_rest():
+        for chunk in chunks:
+            chunk.load()
+        up_loads.append(fetch(up_hbm, shared["up"]))
+        for row in range(2):
+            for place, (dx, half) in enumerate(PLACES):
+                first = aligned(here.owner((here.yl + 1 - row) % 2, dx) * 2 + half, HALF)
+                down_loads.append(
+                    fetch(
+                        down_hbm.at[pl.ds(first, HALF)],
+                        shared["down"].at[pl.ds(row * ROW + place * HALF, HALF)],
+                    )
+                )
+
+    shared.update(load_rest=load_rest)
     chunks = [Chunk(i, net, here, scratch["chunks"][i], shared) for i in range(len(CHUNKS))]
-    chunks[0].load()
-    up_load = fetch(up_hbm, shared["up"])
-    down_loads = []
-    for row in range(2):
-        for place, (dx, half) in enumerate(PLACES):
-            first = aligned(here.owner((here.yl + 1 - row) % 2, dx) * 2 + half, HALF)
-            down_loads.append(
-                fetch(
-                    down_hbm.at[pl.ds(first, HALF)],
-                    shared["down"].at[pl.ds(row * ROW + place * HALF, HALF)],
-                )
-            )
-    for chunk in chunks[1:]:
-        chunk.load()
-
     natural = down_grad
 
     def turn_down():
@@ -651,7 +674,7 @@
             copy.wait()
 
     def turn_up():
-        up_load.wait()
+        up_loads[0].wait()
         for i in range(4):
             part = pl.ds(i * 384, 384)
             natural[part, :] = shared["up"][:, part].T
@@ -661,13 +684,7 @@
                 shared["up_t"][pl.ds(row * ROW + place * HALF, HALF)] = natural[pl.ds(source, HALF)]
 
     shared.update(turn_up=turn_up, turn_down=turn_down)
-    barrier = pltpu.get_barrier_semaphore()
-    partners = [here.dev(dc=1), here.dev(dyl=1), here.dev(dx=1), here.dev(dx=3)]
-    partners += [here.dev(dyh=dyh, dz=dz) for dyh in range(2) for dz in range(4) if dyh or dz]
-    for device in partners:
-        pl.semaphore_signal(barrier, inc=1, device_id=device, device_id_type=MESH)
     pl.semaphore_wait(barrier, len(partners))
-
     for step in order(chunks):
         step()
     for chunk in chunks:

time: 127 us -> 127 us (level)
  no operation moved by 1% of the time
where the time goes in v5:
time: 127 us
  Pallas kernels  126 us (99%)
    pallas_call x1, Pallas kernels, body(): pl.pallas_call(run, out_shape=(pltpu.VMEM((HALF, 640), BF16), pltpu.VMEM(...  124 us

profile of v5, /device:TPU:0, one launch (start us, length us, event | category | flops | bytes accessed | tf_op | source)
XLA Modules:
  0.0 126.9 jit_solution(9999792372591636251)
XLA Ops:
  0.6 123.8 %mlp_backward.1 = (bf16[96,640]{1,0:T(8,128)(2,1)S(1)}, bf16[768,1536]{1,0:T(8,128)(2,1)S(1)}, bf16[1536,768]{1,0:T(8,128)(2,1)S(1)}) custom-call(bf16[96,640]{1,0:T(8,128)(2,1)} %bitcast.3, bf16[96,640]{1,0:T(8,128)(2,1)} %bitcast.4, bf16[768,1536]{1,0:T(8,128)(2,1)} %refs_2_.1, bf16[1536,768]{1,0:T(8,128)(2,1)} %refs_3_.1), custom_call_target="tpu_custom_call" | custom-call | flops 15100000256 | bytes 10000000 | tf_op jit(solution)/shard_map/mlp_backward/pallas_call | solution.py:725
  124.5 2.3 %hand_over.1 = (bf16[96,640]{1,0:T(8,128)(2,1)}, bf16[768,1536]{1,0:T(8,128)(2,1)}, bf16[1536,768]{1,0:T(8,128)(2,1)}) custom-call(bf16[96,640]{1,0:T(8,128)(2,1)S(1)} %get-tuple-element.9.refs_0_, bf16[768,1536]{1,0:T(8,128)(2,1)S(1)} %get-tuple-element.10.refs_1_, bf16[1536,768]{1,0:T(8,128)(2,1)S(1)} %get-tuple-element.11.refs_2_), custom_call_target="tpu_custom_call" | custom-call | tf_op jit(solution)/shard_map/hand_over/pallas_call | solution.py:743
